TPU v7x, 512 devices: a whole 4x4x16 slice. The times are simulated.
512 devices in a mesh: row: 8 (over z_lo), inst: 16 (over y, z_hi, core), cell: 4 (over x).
Axes of the slice: x: 4, y: 4, z: 16 (z_hi: 2, z_lo: 8; z = z_hi * 8 + z_lo), core: 2. Of those that a mesh axis runs over, the one named last changes fastest.
Arguments:
- base_state: float32 [4, 64, 512, 512], P(None, 'inst', 'row', 'cell'), as said below
- segment_state: float32 [4, 64, 512, 512], P(None, 'inst', 'row', 'cell'), as said below
- spectral: float32 [8, 64, 64], P('row'), as said below
- donors: int32 [8, 2, 64, 2], P('row'), may hold values from 0 to 63, as said below
- donor_weight: float32 [8, 2, 64], P('row'), may hold values from 0 to 1
Outputs:
- new_state: float32 [4, 64, 512, 512], P(None, 'inst', 'row', 'cell')
- residual: float32 [4, 64, 512, 512], P(None, 'inst', 'row', 'cell')
Inputs may be any that keep to these rules, and one draw needn't show every extreme that they name: Every cell and slot of base_state and segment_state holds a state (rho, rho u, rho v, E) with rho between 0.75 and 1.25 and pressure between 0.35 and 0.95. `segment_state`: as for base_state. spectral[s] is the frequency of blade row b(s) times the spectral time-derivative matrix over its first n(s) slots, zero in all other rows and columns; sections of one blade row have equal matrices. Side 0 refers to section s-1, side 1 to section s+1. Where that section belongs to another blade row and j < n(s), both donors are slots below that row's count; otherwise both donors equal j.
All inputs are finite; a program needn't handle non-finite values.
Results may differ from a plain program's by a relative error of at most 0.0003.
Values sent between devices are 32-bit elements; how exact they have to be, the bound alone decides.
No kernel may reach another device: no remote copies, remote signals or barrier semaphores. Data moves between devices by JAX's collectives and lax.ppermute only.
A program may use at most 64 MiB of HBM per device.

v0:
```python
import jax
import jax.numpy as jnp
from jax import lax
from jax.sharding import PartitionSpec as P

heat_ratio = 1.4
courant = 0.8
segment_coeff = 0.5


def extended_2(value, sides, width, wrap):
    for axis, dim in sides:
        devices, length = (lax.axis_size(axis), value.shape[dim])
        up = [(i, (i + 1) % devices) for i in range(devices if wrap else devices - 1)]
        down = [(j, i) for i, j in up]
        last = lax.slice_in_dim(value, length - width, length, axis=dim)
        first = lax.slice_in_dim(value, 0, width, axis=dim)
        before = lax.ppermute(last, axis, up)
        after = lax.ppermute(first, axis, down)
        value = jnp.concatenate([before, value, after], axis=dim)
    return value


def primitives(conserved):
    density = conserved[0]
    axial_vel = conserved[1] / density
    cross_vel = conserved[2] / density
    pressure = (heat_ratio - 1.0) * (
        conserved[3] - 0.5 * density * (axial_vel * axial_vel + cross_vel * cross_vel)
    )
    return (density, axial_vel, cross_vel, pressure)


def roe_flux(left_state, right_state):
    dens_left, norm_left, tang_left, pres_left = primitives(left_state)
    dens_right, norm_right, tang_right, pres_right = primitives(right_state)
    enth_left = (left_state[3] + pres_left) / dens_left
    enth_right = (right_state[3] + pres_right) / dens_right
    root_left = jnp.sqrt(dens_left)
    root_right = jnp.sqrt(dens_right)
    weight = 1.0 / (root_left + root_right)
    norm_avg = (root_left * norm_left + root_right * norm_right) * weight
    tang_avg = (root_left * tang_left + root_right * tang_right) * weight
    enth_avg = (root_left * enth_left + root_right * enth_right) * weight
    dens_avg = root_left * root_right
    kinetic = 0.5 * (norm_avg * norm_avg + tang_avg * tang_avg)
    celerity_sq = (heat_ratio - 1.0) * (enth_avg - kinetic)
    celerity = jnp.sqrt(celerity_sq)
    jump_dens = dens_right - dens_left
    jump_norm = norm_right - norm_left
    jump_tang = tang_right - tang_left
    jump_pres = pres_right - pres_left
    wave_one = (jump_pres - dens_avg * celerity * jump_norm) / (2.0 * celerity_sq)
    wave_four = (jump_pres + dens_avg * celerity * jump_norm) / (2.0 * celerity_sq)
    wave_two = jump_dens - jump_pres / celerity_sq
    wave_three = dens_avg * jump_tang
    speed_one = jnp.abs(norm_avg - celerity) * wave_one
    speed_two = jnp.abs(norm_avg) * wave_two
    speed_three = jnp.abs(norm_avg) * wave_three
    speed_four = jnp.abs(norm_avg + celerity) * wave_four
    mass_left = dens_left * norm_left
    mass_right = dens_right * norm_right
    acoustic = speed_one + speed_two + speed_four
    flux_mass = 0.5 * (mass_left + mass_right) - 0.5 * acoustic
    flux_norm = 0.5 * (
        mass_left * norm_left + pres_left + mass_right * norm_right + pres_right
    ) - 0.5 * (
        speed_one * (norm_avg - celerity)
        + speed_two * norm_avg
        + speed_four * (norm_avg + celerity)
    )
    flux_tang = 0.5 * (mass_left * tang_left + mass_right * tang_right) - 0.5 * (
        acoustic * tang_avg + speed_three
    )
    flux_energy = 0.5 * (mass_left * enth_left + mass_right * enth_right) - 0.5 * (
        speed_one * (enth_avg - norm_avg * celerity)
        + speed_two * kinetic
        + speed_three * tang_avg
        + speed_four * (enth_avg + norm_avg * celerity)
    )
    return jnp.stack([flux_mass, flux_norm, flux_tang, flux_energy])


def reorder(conserved):
    return jnp.stack([conserved[0], conserved[2], conserved[1], conserved[3]])


def per_device(base_state, segment_state, spectral, donors, donor_weight):
    highest = lax.Precision.HIGHEST
    sections = lax.axis_size("row")
    section = lax.axis_index("row")
    inst_count = segment_state.shape[1]
    slot_count = spectral.shape[1]
    first_inst = lax.axis_index("inst") * inst_count
    blade_row = (section >= sections // 4).astype(jnp.int32) + (
        section >= 3 * sections // 4
    ).astype(jnp.int32)
    active = jnp.where(blade_row == 0, 45, jnp.where(blade_row == 1, 64, 55))
    targets = first_inst + jnp.arange(inst_count, dtype=jnp.int32)
    live_mask = (targets < active)[None, :, None, None]
    columns = jnp.arange(slot_count, dtype=jnp.int32)
    donor_low = donors[0, :, :, 0]
    donor_high = donors[0, :, :, 1]
    fraction = donor_weight[0]
    resample = (1.0 - fraction)[:, :, None] * (
        columns[None, None, :] == donor_low[:, :, None]
    ).astype(jnp.float32) + fraction[:, :, None] * (
        columns[None, None, :] == donor_high[:, :, None]
    ).astype(
        jnp.float32
    )
    padded = extended_2(segment_state, (("row", 2),), 1, False)
    from_up = padded[:, :, 0, :]
    from_down = padded[:, :, -1, :]
    local_rows = lax.dynamic_slice_in_dim(resample, first_inst, inst_count, 1)
    matrix_part = local_rows
    upper_sum = jnp.einsum(
        "jl,vlp->vjp",
        matrix_part[0],
        lax.all_gather(from_up, "inst", axis=1, tiled=True),
        precision=highest,
    )
    lower_sum = jnp.einsum(
        "jl,vlp->vjp",
        matrix_part[1],
        lax.all_gather(from_down, "inst", axis=1, tiled=True),
        precision=highest,
    )
    ghost_up = upper_sum
    ghost_down = lower_sum
    first_row = segment_state[:, :, 0, :]
    last_row = segment_state[:, :, -1, :]
    ghost_up = jnp.where(section == 0, first_row, ghost_up)
    ghost_down = jnp.where(section == sections - 1, last_row, ghost_down)
    extended = jnp.concatenate(
        [ghost_up[:, :, None], segment_state, ghost_down[:, :, None]], axis=2
    )
    axial_flux = roe_flux(extended[:, :, :-1], extended[:, :, 1:])
    axial_net = axial_flux[:, :, 1:] - axial_flux[:, :, :-1]
    beside_all = extended_2(segment_state, (("cell", 3),), 1, True)
    pitch_flux = reorder(roe_flux(reorder(beside_all[..., :-1]), reorder(beside_all[..., 1:])))
    pitch_net = pitch_flux[..., 1:] - pitch_flux[..., :-1]
    spatial = axial_net + pitch_net
    spectral_rows = lax.dynamic_slice_in_dim(spectral[0], first_inst, inst_count, 0)
    matrix_part = spectral_rows
    temporal = jnp.einsum(
        "jl,vlap->vjap",
        matrix_part,
        lax.all_gather(segment_state, "inst", axis=1, tiled=True),
        precision=highest,
    )
    residual = jnp.where(live_mask, temporal + spatial, 0.0)
    density, axial_vel, cross_vel, pressure = primitives(segment_state)
    celerity = jnp.sqrt(heat_ratio * pressure / density)
    time_step = courant / (jnp.abs(axial_vel) + jnp.abs(cross_vel) + 2.0 * celerity)
    updated = base_state - segment_coeff * time_step * residual
    return (updated, residual)


def solution(mesh):
    placed = (
        P(None, "inst", "row", "cell"),
        P(None, "inst", "row", "cell"),
        P("row", None, None),
        P("row", None, None, None),
        P("row", None, None),
    )
    return jax.shard_map(
        per_device,
        mesh=mesh,
        in_specs=placed,
        out_specs=(P(None, "inst", "row", "cell"), P(None, "inst", "row", "cell")),
        check_vma=False,
    )
```

profile of v0, /device:TPU:1, one launch (start us, length us, event | category | flops | bytes accessed | tf_op | source)
XLA Modules:
  0.0 220.9 jit_solution(18184517973960341778)
XLA Ops:
  7.2 1.9 copy.38
  9.2 0.9 fusion.41
  10.1 4.4 %collective-permute-start = (f32[4,4,1,128]{3,1,0,2:T(4,128)S(1)}, f32[4,4,1,128]{3,1,0,2:T(4,128)S(1)}, u32[]{:S(2)}, u32[]{:S(2)}) collective-permute-start(f32[4,4,1,128]{3,1,0,2:T(4,128)S(1)} %bitcast.52), channel_id=1, source_target_pairs={{0,64},{64,128},{128,192},{192,256},{256,320},{320,384},{384,448},... | collective-permute-start | bytes 24584 | tf_op jit(solution)/shard_map/ppermute | solution.py:18
  14.5 1.3 collective-permute-start.1
  15.8 2.2 fusion.42
  17.9 3.1 %collective-permute-start.2 = (f32[4,4,64,1]{3,2,1,0:T(8,128)S(1)}, f32[4,4,64,1]{3,2,1,0:T(8,128)S(1)}, u32[]{:S(2)}, u32[]{:S(2)}) collective-permute-start(f32[4,4,64,1]{3,2,1,0:T(8,128)S(1)} %get-tuple-element.31), channel_id=1, source_target_pairs={{0,1},{1,2},{2,3},{3,0},{4,5},{5,6},{6,7},{7,4},{8,9},{9,10},{10,1... | collective-permute-start | bytes 12296 | tf_op jit(solution)/shard_map/ppermute | solution.py:18
  21.1 3.4 %collective-permute-start.3 = (f32[4,4,64,1]{3,2,1,0:T(8,128)}, f32[4,4,64,1]{3,2,1,0:T(8,128)S(1)}, u32[]{:S(2)}, u32[]{:S(2)}) collective-permute-start(f32[4,4,64,1]{3,2,1,0:T(8,128)} %get-tuple-element.32), channel_id=1, source_target_pairs={{1,0},{2,1},{3,2},{0,3},{5,4},{6,5},{7,6},{4,7},{9,8},{10,9},{11,1... | collective-permute-start | bytes 12296 | tf_op jit(solution)/shard_map/ppermute | solution.py:19
  24.5 0.7 broadcast_subtract_fusion
  25.1 0.8 constant_dynamic-slice_fusion
  25.9 0.8 fusion.43
  26.7 1.1 constant_dynamic-update-slice_fusion.1
  27.9 1.2 multiply_bitcast_fusion
  29.1 4.8 %collective-permute-done.3 = f32[4,4,64,1]{3,2,1,0:T(8,128)S(1)} collective-permute-done((f32[4,4,64,1]{3,2,1,0:T(8,128)}, f32[4,4,64,1]{3,2,1,0:T(8,128)S(1)}, u32[]{:S(2)}, u32[]{:S(2)}) %collective-permute-start.3) | collective-permute-done | bytes 4128 | tf_op jit(solution)/shard_map/ppermute | solution.py:19
  34.0 2.1 multiply_subtract_fusion.4
  36.1 1.5 multiply_subtract_fusion.2
  37.7 53.8 %all-gather.1 = f32[4,64,1,128]{3,0,2,1:T(4,128)S(1)} all-gather(f32[4,4,1,128]{3,0,2,1:T(4,128)S(1)} %copy.45), channel_id=3, replica_groups=mesh['row'=8,'inst'=16,'cell'=4] {'inst'}, dimensions={1}, use_global_device_ids=true | all-gather | bytes 139264 | tf_op jit(solution)/shard_map/all_gather | solution.py:126
  91.5 50.4 %all-gather = f32[4,64,1,128]{3,0,2,1:T(4,128)S(1)} all-gather(f32[4,4,1,128]{3,0,2,1:T(4,128)S(1)} %copy.43), channel_id=2, replica_groups=mesh['row'=8,'inst'=16,'cell'=4] {'inst'}, dimensions={1}, use_global_device_ids=true | all-gather | bytes 139264 | tf_op jit(solution)/shard_map/all_gather | solution.py:120
  141.9 0.2 fusion.2
  142.1 0.2 fusion.3
  142.3 0.5 multiply_subtract_fusion.8
  142.8 0.8 multiply_subtract_fusion.7
  143.6 57.2 %all-gather.4.cloned.1.call-done = f32[4,64,64,128]{3,2,0,1:T(8,128)} async-done(((f32[4,4,64,128]{3,2,0,1:T(8,128)}), f32[4,64,64,128]{3,2,0,1:T(8,128)}) %all-gather.4.cloned.1.call-update) | async-done | bytes 8388624 | tf_op jit(solution)/shard_map/all_gather | solution.py:149
  200.8 12.0 %fusion = f32[4,4,64,128]{3,0,2,1:T(4,128)S(1)} fusion(f32[4,64,64,128]{3,2,0,1:T(8,128)} %all-gather.4.cloned.1.call-done, f32[1,64,64]{2,1,0:T(8,128)S(1)} %copy-done, s32[]{:T(128)S(6)} %select_n.32), kind=kOutput, calls=%fused_computation | convolution fusion | flops 100663296 | bytes 8914948 | tf_op jit(solution)/shard_map/jl,vlap->vjap/dot_general | solution.py:146
  212.8 1.2 multiply_subtract_fusion
  (19 shorter events, 0.4 us)
Async XLA Ops:
  7.2 193.6 %copy-start = (f32[1,64,64]{2,1,0:T(8,128)S(1)}, f32[1,64,64]{2,1,0:T(8,128)}, u32[]{:S(2)}) copy-start(f32[1,64,64]{2,1,0:T(8,128)} %param.7) | copy-start | bytes 49156
  7.2 29.0 %copy-start.1 = (f32[4,4,64,128]{3,2,1,0:T(8,128)S(1)}, f32[4,4,64,128]{3,2,1,0:T(8,128)}, u32[]{:S(2)}) copy-start(f32[4,4,64,128]{3,2,1,0:T(8,128)} %param.6) | copy-start | bytes 1572868
  7.2 193.6 %all-gather.4.cloned.1.call-start = ((), (), s32[]{:S(2)}) async-start(), calls=%async_computation | async-start | bytes 8912896 | tf_op jit(solution)/shard_map/all_gather | solution.py:149
  10.1 27.6 %collective-permute-start = (f32[4,4,1,128]{3,1,0,2:T(4,128)S(1)}, f32[4,4,1,128]{3,1,0,2:T(4,128)S(1)}, u32[]{:S(2)}, u32[]{:S(2)}) collective-permute-start(f32[4,4,1,128]{3,1,0,2:T(4,128)S(1)} %bitcast.52), channel_id=1, source_target_pairs={{0,64},{64,128},{128,192},{192,256},{256,320},{320,384},{384,448},... | collective-permute-start | bytes 24584 | tf_op jit(solution)/shard_map/ppermute | solution.py:18
  14.5 23.2 %collective-permute-start.1 = (f32[4,4,1,128]{3,1,0,2:T(4,128)S(1)}, f32[4,4,1,128]{3,1,0,2:T(4,128)S(1)}, u32[]{:S(2)}, u32[]{:S(2)}) collective-permute-start(f32[4,4,1,128]{3,1,0,2:T(4,128)S(1)} %bitcast.50), channel_id=1, source_target_pairs={{64,0},{128,64},{192,128},{256,192},{320,256},{384,320},{448,384},... | collective-permute-start | bytes 24584 | tf_op jit(solution)/shard_map/ppermute | solution.py:19
  17.9 16.1 %collective-permute-start.2 = (f32[4,4,64,1]{3,2,1,0:T(8,128)S(1)}, f32[4,4,64,1]{3,2,1,0:T(8,128)S(1)}, u32[]{:S(2)}, u32[]{:S(2)}) collective-permute-start(f32[4,4,64,1]{3,2,1,0:T(8,128)S(1)} %get-tuple-element.31), channel_id=1, source_target_pairs={{0,1},{1,2},{2,3},{3,0},{4,5},{5,6},{6,7},{7,4},{8,9},{9,10},{10,1... | collective-permute-start | bytes 12296 | tf_op jit(solution)/shard_map/ppermute | solution.py:18
  21.1 12.9 %collective-permute-start.3 = (f32[4,4,64,1]{3,2,1,0:T(8,128)}, f32[4,4,64,1]{3,2,1,0:T(8,128)S(1)}, u32[]{:S(2)}, u32[]{:S(2)}) collective-permute-start(f32[4,4,64,1]{3,2,1,0:T(8,128)} %get-tuple-element.32), channel_id=1, source_target_pairs={{1,0},{2,1},{3,2},{0,3},{5,4},{6,5},{7,6},{4,7},{9,8},{10,9},{11,1... | collective-permute-start | bytes 12296 | tf_op jit(solution)/shard_map/ppermute | solution.py:19
  37.6 175.2 %copy-start.2 = (f32[4,4,64,128]{3,2,1,0:T(8,128)S(1)}, f32[4,4,64,128]{3,2,1,0:T(8,128)}, u32[]{:S(2)}) copy-start(f32[4,4,64,128]{3,2,1,0:T(8,128)} %param.5) | copy-start | bytes 1572868
Sparse Core Ops, SparseCore 0:
  11.9 188.8 all-gather.3
where the time goes:
time: 221 us
  blocking collectives  104 us (47%)
  waiting for transfers between devices  62 us (28%)
  between operations  14.2 us (6%)
  matrix products  12.4 us (6%)
  starting transfers between devices  12.2 us (6%)
  other arithmetic  8.18 us (4%)
  local copies, waits for them, and re-layouts  7.73 us (3%)
    all_gather x1, waiting for transfers between devices, per_device(): lax.all_gather(segment_state, 'inst', axis=1, tiled=True)  57.2 us
    all_gather x1, blocking collectives, per_device(): lax.all_gather(from_down, 'inst', axis=1, tiled=True)  53.8 us
    all_gather x1, blocking collectives, per_device(): lax.all_gather(from_up, 'inst', axis=1, tiled=True)  50.4 us
    dot_general x1, matrix products, per_device(): jnp.einsum('jl,vlap->vjap', matrix_part, lax.all_gather(segment_state, 'i...  12 us
    ppermute x2, starting transfers between devices, extended_2(): before = lax.ppermute(last, axis, up)  7.48 us
    ppermute x2, waiting for transfers between devices, extended_2(): after = lax.ppermute(first, axis, down)  4.84 us
    ppermute x2, starting transfers between devices, extended_2(): after = lax.ppermute(first, axis, down)  4.67 us
  transfers between devices with their start and end apart: 5, of which 2 were waited for; matrix products, arithmetic and copies ran while one was open for 6% of the time, Pallas kernels for 0%

commit v1 on v0

v1 whole, which is shorter than its diff:
```python
import jax
import jax.numpy as jnp
from jax import lax
from jax.experimental import pallas as pl
from jax.experimental.pallas import tpu as pltpu
from jax.sharding import PartitionSpec as P

heat_ratio = 1.4
courant = 0.8
segment_coeff = 0.5

GROUPS = [[y * 4 + half * 2 + c for y in range(4) for c in range(2)] for half in range(2)]
PARTNER = [(i, i ^ 2) for i in range(16)]
INTERFACE = (1, 2, 5, 6)
VMEM = pl.BlockSpec(memory_space=pltpu.VMEM)
SMEM = pl.BlockSpec(memory_space=pltpu.SMEM)


def swap_members(value):
    return lax.all_to_all(value, "inst", 0, 0, tiled=True, axis_index_groups=GROUPS)


def primitives(dens, mom_norm, mom_tang, energy):
    inverse = 1.0 / dens
    norm = mom_norm * inverse
    tang = mom_tang * inverse
    pres = (heat_ratio - 1.0) * (energy - 0.5 * (mom_norm * norm + mom_tang * tang))
    enth = (energy + pres) * inverse
    return (dens, norm, tang, pres, enth, jnp.sqrt(dens), mom_norm)


def roe(left, right):
    dens_l, norm_l, tang_l, pres_l, enth_l, root_l, mass_l = left
    dens_r, norm_r, tang_r, pres_r, enth_r, root_r, mass_r = right
    weight = 1.0 / (root_l + root_r)
    share_l = root_l * weight
    share_r = root_r * weight
    norm = share_l * norm_l + share_r * norm_r
    tang = share_l * tang_l + share_r * tang_r
    enth = share_l * enth_l + share_r * enth_r
    dens = root_l * root_r
    kinetic = 0.5 * (norm * norm + tang * tang)
    cel_sq = (heat_ratio - 1.0) * (enth - kinetic)
    cel = jnp.sqrt(cel_sq)
    inverse = 1.0 / cel_sq
    jump_pres = pres_r - pres_l
    push = dens * cel * (norm_r - norm_l)
    half_inverse = 0.5 * inverse
    one = jnp.abs(norm - cel) * ((jump_pres - push) * half_inverse)
    four = jnp.abs(norm + cel) * ((jump_pres + push) * half_inverse)
    speed = jnp.abs(norm)
    two = speed * ((dens_r - dens_l) - jump_pres * inverse)
    three = speed * (dens * (tang_r - tang_l))
    outer = one + four
    acoustic = outer + two
    spread = cel * (four - one)
    flux_mass = 0.5 * (mass_l + mass_r - acoustic)
    flux_norm = 0.5 * (mass_l * norm_l + pres_l + mass_r * norm_r + pres_r - (acoustic * norm + spread))
    flux_tang = 0.5 * (mass_l * tang_l + mass_r * tang_r - (acoustic * tang + three))
    flux_energy = 0.5 * (
        mass_l * enth_l + mass_r * enth_r - (outer * enth + norm * spread + two * kinetic + three * tang)
    )
    return flux_mass, flux_norm, flux_tang, flux_energy


def operator_rows(matrix, source, first_row, variables, begin, store):
    for pair in range(4):
        targets = [(member, i) for member in (2 * pair, 2 * pair + 1) for i in range(4)]

        def body(member, sums):
            sums = list(sums)
            for i in range(4):
                tiles = [source[member, pl.ds(first_row + (v * 4 + i) * 8, 8), :] for v in range(variables)]
                for k, (tm, ti) in enumerate(targets):
                    factor = matrix[tm * 4 + ti, member * 4 + i]
                    for v in range(variables):
                        sums[k * variables + v] = sums[k * variables + v] + factor * tiles[v]
            return tuple(sums)

        start = tuple(begin(tm, v, ti) for tm, ti in targets for v in range(variables))
        sums = lax.fori_loop(0, 8, body, start)
        for k, (tm, ti) in enumerate(targets):
            for v in range(variables):
                store(tm, v, ti, sums[k * variables + v])


def outgoing_kernel(matrix, source, out):
    def store(member, v, i, tile):
        out[member, pl.ds((v * 4 + i) * 8, 8), :] = tile

    operator_rows(matrix, source, 64, 2, lambda *_: jnp.zeros((8, 128), jnp.float32), store)


def own_kernel(matrix, source, out):
    for first in (0, 64):

        def store(member, v, i, tile, first=first):
            out[member, pl.ds(first + (v * 4 + i) * 8, 8), :] = tile

        operator_rows(matrix, source, first, 2, lambda *_: jnp.zeros((8, 128), jnp.float32), store)


def arrived_kernel(matrix, resample, own, source, out):
    def begin(member, v, i):
        return own[member, pl.ds((v * 4 + i) * 8, 8), :]

    def store(member, v, i, tile):
        out[member, pl.ds((v * 4 + i) * 8, 8), :] = tile

    operator_rows(matrix, source, 0, 2, begin, store)
    for member in range(8):
        out[member, 64:128, :] = own[member, 64:128, :]
    edges = source[:, 64:72, :].reshape(64, 128)
    ghost = jnp.dot(resample[...], edges, precision=lax.Precision.HIGHEST, preferred_element_type=jnp.float32)
    out[:, 128:136, :] = ghost.reshape(8, 8, 128)


def spatial_kernel(state, sides, out, step, prims):
    lane = lax.broadcasted_iota(jnp.int32, (8, 128), 1)
    row = lax.broadcasted_iota(jnp.int32, (8, 128), 0)
    columns = sides[0].T
    for o in range(8):
        at = slice(8 * o, 8 * o + 8)
        cells = [state[v, 0, at, :] for v in range(4)]
        dens, norm, tang, pres, enth, root, _ = primitives(*cells)
        cel = jnp.sqrt(heat_ratio * pres / dens)
        step[0, at, :] = (segment_coeff * courant) / (jnp.abs(norm) + jnp.abs(tang) + 2.0 * cel)
        for k, value in enumerate((dens, norm, tang, pres, enth, root, cells[1], cells[2])):
            prims[k, at, :] = value
    previous = None
    for o in range(8):
        at = slice(8 * o, 8 * o + 8)
        here = [prims[k, at, :] for k in range(8)]
        if o < 7:
            below = [prims[k, 8 * o + 1 : 8 * o + 9, :] for k in range(8)]
        else:
            below = [pltpu.roll(x, 7, 0) for x in here]
        axial = roe([here[k] for k in (0, 1, 2, 3, 4, 5, 6)], [below[k] for k in (0, 1, 2, 3, 4, 5, 6)])
        if o == 7:
            axial = [jnp.where(row == 7, 0.0, x) for x in axial]
        ahead = [pltpu.roll(x, 127, 1) for x in here]
        mass, tang, norm, energy = roe(
            [here[k] for k in (0, 2, 1, 3, 4, 5, 7)], [ahead[k] for k in (0, 2, 1, 3, 4, 5, 7)]
        )
        pitch = (mass, norm, tang, energy)
        shifted = [pltpu.roll(x, 1, 0) for x in axial]
        for v in range(4):
            above = 0.0 if previous is None else jnp.broadcast_to(previous[v][0:1, :], (8, 128))
            net = axial[v] - jnp.where(row == 0, above, shifted[v])
            first = jnp.broadcast_to(columns[at, 2 * v : 2 * v + 1], (8, 128))
            last = jnp.broadcast_to(columns[at, 2 * v + 1 : 2 * v + 2], (8, 128))
            after = jnp.where(lane == 127, last, pitch[v])
            before = jnp.where(lane == 0, first, pltpu.roll(pitch[v], 1, 1))
            out[v, 0, at, :] = net + (after - before)
        previous = shifted


def final_kernel(facts, base, state, spatial, step, local, crossed, new_state, residual):
    row = lax.broadcasted_iota(jnp.int32, (8, 128), 0)
    first_rows = [state[v, :, 0, :] for v in range(4)]
    last_rows = [state[v, :, 63, :] for v in range(4)]
    up = [jnp.where(facts[1] == 1, first_rows[v], local[2 * v, 128:132, :]) for v in range(4)]
    down = [jnp.where(facts[2] == 1, last_rows[v], local[2 * v + 1, 128:132, :]) for v in range(4)]
    flux_up = roe(primitives(*up), primitives(*first_rows))
    flux_down = roe(primitives(*last_rows), primitives(*down))
    for i in range(4):
        live = facts[0] > i
        for o in range(8):
            at = slice(8 * o, 8 * o + 8)
            factor = step[i, at, :]
            for v in range(4):
                rows = slice((v * 4 + i) * 8, (v * 4 + i) * 8 + 8)
                total = spatial[v, i, at, :] + local[o, rows, :]
                if v >= 2:
                    total = total + crossed[o, slice(rows.start - 64, rows.stop - 64), :]
                if o == 0:
                    edge = jnp.broadcast_to(flux_up[v][i : i + 1, :], (8, 128))
                    total = total - jnp.where(row == 0, edge, 0.0)
                if o == 7:
                    edge = jnp.broadcast_to(flux_down[v][i : i + 1, :], (8, 128))
                    total = total + jnp.where(row == 7, edge, 0.0)
                total = jnp.where(live, total, 0.0)
                residual[v, i, at, :] = total
                new_state[v, i, at, :] = base[v, i, at, :] - factor * total


def shape(*dims):
    return jax.ShapeDtypeStruct(dims, jnp.float32)


def cost(flops, moved):
    return pl.CostEstimate(flops=flops, bytes_accessed=moved, transcendentals=0)


def per_device(base_state, segment_state, spectral, donors, donor_weight):
    section = lax.axis_index("row")
    inst = lax.axis_index("inst")
    half = (inst // 2) % 2
    member = (inst // 4) * 2 + inst % 2
    blade_row = (section >= 2).astype(jnp.int32) + (section >= 6).astype(jnp.int32)
    active = jnp.where(blade_row == 0, 45, jnp.where(blade_row == 1, 64, 55))
    facts = jnp.stack([active - 4 * inst, (section == 0).astype(jnp.int32), (section == 7).astype(jnp.int32)])

    blocks = spectral[0].reshape(4, 2, 8, 4, 2, 8)
    low_low, low_high, high_low, high_high = [
        blocks[:, a, :, :, b, :].reshape(32, 32) for a in range(2) for b in range(2)
    ]
    own_own = jnp.where(half == 0, low_low, high_high)
    own_partner = jnp.where(half == 0, low_high, high_low)
    partner_own = jnp.where(half == 0, high_low, low_high)

    side = member % 2
    pairs = jnp.where(side == 0, donors[0, 0], donors[0, 1]).reshape(4, 2, 2, 4, 2)
    pairs = jnp.where(half == 0, pairs[:, 0], pairs[:, 1]).reshape(8, 4, 2)
    part = jnp.where(side == 0, donor_weight[0, 0], donor_weight[0, 1]).reshape(4, 2, 2, 4)
    part = jnp.where(half == 0, part[:, 0], part[:, 1]).reshape(8, 4)
    k = jnp.arange(64, dtype=jnp.int32)
    source_member, relative, source_i = k // 8, (k // 4) % 2, k % 4
    slots = (source_member // 2) * 16 + (half ^ relative) * 8 + (source_member % 2) * 4 + source_i
    resample = (1.0 - part)[..., None] * (slots == pairs[..., 0, None]).astype(jnp.float32) + part[..., None] * (
        slots == pairs[..., 1, None]
    ).astype(jnp.float32)
    resample = jnp.pad(resample, ((0, 0), (0, 4), (0, 0))).reshape(64, 64)

    octets = segment_state.reshape(4, 4, 8, 8, 128).transpose(2, 0, 1, 3, 4).reshape(8, 128, 128)
    mixed = swap_members(octets)
    raw_half = octets[:, :64]
    arrived_half = lax.ppermute(raw_half, "inst", PARTNER)

    first_row = segment_state[:, :, 0, :]
    last_row = segment_state[:, :, 63, :]
    upward = [(i, i + 1) for i in range(7)]
    downward = [(i + 1, i) for i in range(7)]
    from_up = lax.ppermute(last_row, "row", upward)
    from_down = lax.ppermute(first_row, "row", downward)
    edges = jnp.stack([from_up, from_down], axis=1).reshape(8, 4, 128)
    partner_edges = lax.ppermute(
        edges, ("row", "inst"), [(r * 16 + a, r * 16 + b) for r in INTERFACE for a, b in PARTNER]
    )

    outgoing = pl.pallas_call(
        outgoing_kernel, out_shape=shape(8, 64, 128), in_specs=[SMEM, VMEM], out_specs=VMEM,
        cost_estimate=cost(4 << 20, 1 << 20), name="outgoing",
    )(partner_own, mixed)
    crossed = lax.ppermute(swap_members(outgoing), "inst", PARTNER)
    own = pl.pallas_call(
        own_kernel, out_shape=shape(8, 128, 128), in_specs=[SMEM, VMEM], out_specs=VMEM,
        cost_estimate=cost(8 << 20, 1 << 20), name="own",
    )(own_own, mixed)

    first_column = segment_state[..., 0]
    last_column = segment_state[..., 127]
    around = [(i, (i + 1) % 4) for i in range(4)]
    from_left = lax.ppermute(last_column, "cell", around)
    from_right = lax.ppermute(first_column, "cell", [(b, a) for a, b in around])

    def swapped(x):
        return primitives(x[0], x[2], x[1], x[3])

    faces = []
    for left, right in ((from_left, first_column), (last_column, from_right)):
        mass, tang, norm, energy = roe(swapped(left), swapped(right))
        faces.append(jnp.stack([mass, norm, tang, energy]))
    sides = jnp.stack(faces, axis=1).transpose(2, 0, 1, 3).reshape(4, 8, 64)
    sides = jnp.pad(sides, ((0, 0), (0, 0), (0, 64)))
    spatial, step = pl.pallas_call(
        spatial_kernel,
        grid=(4,),
        out_shape=(shape(4, 4, 64, 128), shape(4, 64, 128)),
        in_specs=[
            pl.BlockSpec((4, 1, 64, 128), lambda i: (0, i, 0, 0)),
            pl.BlockSpec((1, 8, 128), lambda i: (i, 0, 0)),
        ],
        out_specs=(
            pl.BlockSpec((4, 1, 64, 128), lambda i: (0, i, 0, 0)),
            pl.BlockSpec((1, 64, 128), lambda i: (i, 0, 0)),
        ),
        scratch_shapes=[pltpu.VMEM((8, 64, 128), jnp.float32)],
        cost_estimate=cost(16 << 20, 2 << 20), name="spatial",
    )(segment_state, sides)

    second = swap_members(jnp.concatenate([arrived_half, edges, partner_edges], axis=1))
    totals = pl.pallas_call(
        arrived_kernel, out_shape=shape(8, 136, 128), in_specs=[SMEM, VMEM, VMEM, VMEM], out_specs=VMEM,
        cost_estimate=cost(4 << 20, 1 << 20), name="arrived",
    )(own_partner, resample, own, second)
    local = swap_members(totals)
    return pl.pallas_call(
        final_kernel,
        out_shape=(shape(4, 4, 64, 128), shape(4, 4, 64, 128)),
        in_specs=[SMEM] + [VMEM] * 6,
        out_specs=(VMEM, VMEM),
        cost_estimate=cost(1 << 20, 4 << 20), name="final",
    )(facts, base_state, segment_state, spatial, step, local, crossed)


def solution(mesh):
    placed = (
        P(None, "inst", "row", "cell"),
        P(None, "inst", "row", "cell"),
        P("row", None, None),
        P("row", None, None, None),
        P("row", None, None),
    )
    return jax.shard_map(
        per_device,
        mesh=mesh,
        in_specs=placed,
        out_specs=(P(None, "inst", "row", "cell"), P(None, "inst", "row", "cell")),
        check_vma=False,
    )
```

time: 221 us -> 120 us (0.54)
  the two profiles are of different devices: /device:TPU:1 before, /device:TPU:45 now
where the time goes in v1:
time: 120 us; the launch traced here: 119 us
  starting transfers between devices  61.3 us (51%)
  waiting for transfers between devices  25.6 us (21%)
  Pallas kernels  17.4 us (14%)
  local copies, waits for them, and re-layouts  11.7 us (10%)
  other arithmetic  1.71 us (1%)
    all_to_all x4, starting transfers between devices, swap_members(): lax.all_to_all(value, 'inst', 0, 0, tiled=True, axis_index_groups=GROUPS)  22.4 us
    ppermute x1, starting transfers between devices, per_device(): arrived_half = lax.ppermute(raw_half, 'inst', PARTNER)  14.5 us
    ppermute x1, waiting for transfers between devices, per_device(): crossed = lax.ppermute(swap_members(outgoing), 'inst', PARTNER)  13.5 us
    ppermute x1, waiting for transfers between devices, per_device(): lax.ppermute(edges, ('row', 'inst'), [(r * 16 + a, r * 16 + b) for r in I...  12 us
    ppermute x1, starting transfers between devices, per_device(): crossed = lax.ppermute(swap_members(outgoing), 'inst', PARTNER)  11.7 us
    pallas_call x1, Pallas kernels, per_device(): pl.pallas_call(own_kernel, out_shape=shape(8, 128, 128), in_specs=[SMEM,...  4.21 us
    pallas_call x1, Pallas kernels, per_device(): pl.pallas_call(spatial_kernel, grid=(4,), out_shape=(shape(4, 4, 64, 128)...  4.18 us
    ppermute x1, starting transfers between devices, per_device(): from_up = lax.ppermute(last_row, 'row', upward)  3.55 us
  transfers between devices with their start and end apart: 11, of which 2 were waited for; matrix products, arithmetic and copies ran while one was open for 9% of the time, Pallas kernels for 12%

profile of v1, /device:TPU:45, one launch (start us, length us, event | category | flops | bytes accessed | tf_op | source)
XLA Modules:
  0.0 118.8 jit_solution(11354327034725321099)
XLA Ops:
  0.6 0.9 fusion.46
  1.5 1.9 %collective-permute-start.4 = (f32[4,4,128]{2,1,0:T(4,128)S(1)}, f32[4,4,128]{2,1,0:T(4,128)S(1)}, u32[]{:S(2)}, u32[]{:S(2)}) collective-permute-start(f32[4,4,128]{2,1,0:T(4,128)S(1)} %bitcast.378), channel_id=1, source_target_pairs={{64,0},{128,64},{192,128},{256,192},{320,256},{384,320},{448,384},... | collective-permute-start | bytes 24584 | tf_op jit(solution)/shard_map/ppermute | solution.py:235
  3.5 3.5 %collective-permute-start.3 = (f32[4,4,128]{2,1,0:T(4,128)S(1)}, f32[4,4,128]{2,1,0:T(4,128)S(1)}, u32[]{:S(2)}, u32[]{:S(2)}) collective-permute-start(f32[4,4,128]{2,1,0:T(4,128)S(1)} %bitcast.377), channel_id=1, source_target_pairs={{0,64},{64,128},{128,192},{192,256},{256,320},{320,384},{384,448},... | collective-permute-start | bytes 24584 | tf_op jit(solution)/shard_map/ppermute | solution.py:234
  7.0 1.9 %copy.46 = f32[4,4,8,8,128]{4,3,1,0,2:T(8,128)} copy(f32[4,4,8,8,128]{4,3,2,1,0:T(8,128)} %bitcast.360) | data formatting | bytes 1048576 | tf_op jit(solution)/shard_map/reshape | solution.py:225
  8.9 5.7 %all-to-all-start = ((f32[8,128,128]{2,1,0:T(8,128)}), f32[8,128,128]{2,1,0:T(8,128)S(1)}, u32[]{:S(2)}, u32[]{:S(2)}) async-start(f32[8,128,128]{2,1,0:T(8,128)} %bitcast.23), calls=%async_computation | async-start | bytes 1048576 | tf_op jit(solution)/shard_map/all_to_all | solution.py:20
  14.6 1.0 slice.174
  15.7 14.5 %collective-permute-start.2 = (f32[8,64,128]{2,1,0:T(8,128)S(1)}, f32[8,64,128]{2,1,0:T(8,128)S(1)}, u32[]{:S(2)}, u32[]{:S(2)}) collective-permute-start(f32[8,64,128]{2,1,0:T(8,128)S(1)} %slice.174), channel_id=1, source_target_pairs={{0,8},{4,12},{8,0},{12,4},{16,24},{20,28},{24,16},{28,20},{32,40},... | collective-permute-start | bytes 786440 | tf_op jit(solution)/shard_map/ppermute | solution.py:228
  30.6 2.2 %collective-permute-start.1 = (f32[4,4,64]{2,1,0:T(4,128)S(1)}, f32[4,4,64]{2,1,0:T(4,128)S(1)}, u32[]{:S(2)}, u32[]{:S(2)}) collective-permute-start(f32[4,4,64]{2,1,0:T(4,128)S(1)} %bitcast.375), channel_id=1, source_target_pairs={{1,0},{2,1},{3,2},{0,3},{5,4},{6,5},{7,6},{4,7},{9,8},{10,9},{11,1... | collective-permute-start | bytes 12296 | tf_op jit(solution)/shard_map/ppermute | solution.py:255
  33.0 3.1 %collective-permute-start = (f32[4,4,64]{2,1,0:T(4,128)S(1)}, f32[4,4,64]{2,1,0:T(4,128)S(1)}, u32[]{:S(2)}, u32[]{:S(2)}) collective-permute-start(f32[4,4,64]{2,1,0:T(4,128)S(1)} %bitcast.374), channel_id=1, source_target_pairs={{0,1},{1,2},{2,3},{3,0},{4,5},{5,6},{6,7},{7,4},{8,9},{9,10},{10,1... | collective-permute-start | bytes 12296 | tf_op jit(solution)/shard_map/ppermute | solution.py:254
  38.8 1.9 %collective-permute-start.5 = (f32[8,4,128]{2,1,0:T(4,128)S(1)}, f32[8,4,128]{2,1,0:T(4,128)S(1)}, u32[]{:S(2)}, u32[]{:S(2)}) collective-permute-start(f32[8,4,128]{2,1,0:T(4,128)S(1)} %bitcast.368), channel_id=1, source_target_pairs={{64,72},{68,76},{72,64},{76,68},{80,88},{84,92},{88,80},{92,84},{9... | collective-permute-start | bytes 49160 | tf_op jit(solution)/shard_map/ppermute | solution.py:237
  40.7 12.0 %collective-permute-done.5 = f32[8,4,128]{2,1,0:T(4,128)S(1)} collective-permute-done((f32[8,4,128]{2,1,0:T(4,128)S(1)}, f32[8,4,128]{2,1,0:T(4,128)S(1)}, u32[]{:S(2)}, u32[]{:S(2)}) %collective-permute-start.5) | collective-permute-done | bytes 16416 | tf_op jit(solution)/shard_map/ppermute | solution.py:237
  52.8 0.7 pad_maximum_fusion
  53.5 7.1 %all-to-all-start.1 = ((f32[8,72,128]{2,1,0:T(8,128)}), f32[8,72,128]{2,1,0:T(8,128)S(1)}, u32[]{:S(2)}, u32[]{:S(2)}) async-start(f32[8,72,128]{2,1,0:T(8,128)} %pad_maximum_fusion), calls=%async_computation.1 | async-start | bytes 589824 | tf_op jit(solution)/shard_map/all_to_all | solution.py:20
  62.0 0.7 select_n.164.matrix
  64.8 3.0 %outgoing.1 = f32[8,64,128]{2,1,0:T(8,128)} custom-call(f32[32,32]{1,0:T(8,128)} %select_n.189.matrix, f32[8,128,128]{2,1,0:T(8,128)} %copy-done.1), custom_call_target="tpu_custom_call" | custom-call | flops 4194304 | bytes 1048576 | tf_op jit(solution)/shard_map/outgoing/pallas_call | solution.py:241
  67.7 4.8 %all-to-all-start.3 = ((f32[8,64,128]{2,1,0:T(8,128)}), f32[8,64,128]{2,1,0:T(8,128)S(1)}, u32[]{:S(2)}, u32[]{:S(2)}) async-start(f32[8,64,128]{2,1,0:T(8,128)} %outgoing.1), calls=%async_computation.3 | async-start | bytes 524288 | tf_op jit(solution)/shard_map/all_to_all | solution.py:20
  72.6 4.2 %own.1 = f32[8,128,128]{2,1,0:T(8,128)} custom-call(f32[32,32]{1,0:T(8,128)} %select_n.187.matrix, f32[8,128,128]{2,1,0:T(8,128)} %copy-done.1), custom_call_target="tpu_custom_call" | custom-call | flops 8388608 | bytes 1048576 | tf_op jit(solution)/shard_map/own/pallas_call | solution.py:246
  76.8 3.3 %arrived.1 = f32[8,136,128]{2,1,0:T(8,128)} custom-call(f32[32,32]{1,0:T(8,128)} %select_n.164.matrix, f32[64,64]{1,0:T(8,128)} %pad_bitcast_fusion.resample, f32[8,128,128]{2,1,0:T(8,128)} %own.1, f32[8,72,128]{2,1,0:T(8,128)} %copy-done.3), custom_call_target="tpu_custom_call" | custom-call | flops 4194304 | bytes 1048576 | tf_op jit(solution)/shard_map/arrived/pallas_call | solution.py:283
  80.2 4.8 %all-to-all-start.2 = ((f32[8,136,128]{2,1,0:T(8,128)}), f32[8,136,128]{2,1,0:T(8,128)S(1)}, u32[]{:S(2)}, u32[]{:S(2)}) async-start(f32[8,136,128]{2,1,0:T(8,128)} %arrived.1), calls=%async_computation.2 | async-start | bytes 1114112 | tf_op jit(solution)/shard_map/all_to_all | solution.py:20
  85.0 11.7 %collective-permute-start.6 = (f32[8,64,128]{2,1,0:T(8,128)S(1)}, f32[8,64,128]{2,1,0:T(8,128)S(1)}, u32[]{:S(2)}, u32[]{:S(2)}) collective-permute-start(f32[8,64,128]{2,1,0:T(8,128)S(1)} %all-to-all-done.3), channel_id=1, source_target_pairs={{0,8},{4,12},{8,0},{12,4},{16,24},{20,28},{24,16},{28,20},{32,40},... | collective-permute-start | bytes 786440 | tf_op jit(solution)/shard_map/ppermute | solution.py:245
  97.4 4.2 %spatial.1 = (f32[4,4,64,128]{3,2,1,0:T(8,128)}, f32[4,64,128]{2,1,0:T(8,128)}) custom-call(f32[4,4,64,128]{3,2,1,0:T(8,128)} %state.3, f32[4,8,128]{2,1,0:T(8,128)} %pad.8.sides), custom_call_target="tpu_custom_call" | custom-call | flops 16777216 | bytes 2097152 | tf_op jit(solution)/shard_map/spatial/pallas_call | solution.py:266
  101.6 13.5 %collective-permute-done.6.crossed = f32[8,64,128]{2,1,0:T(8,128)S(1)} collective-permute-done((f32[8,64,128]{2,1,0:T(8,128)S(1)}, f32[8,64,128]{2,1,0:T(8,128)S(1)}, u32[]{:S(2)}, u32[]{:S(2)}) %collective-permute-start.6) | collective-permute-done | bytes 262176 | tf_op jit(solution)/shard_map/ppermute | solution.py:245
  115.1 0.7 copy-done.4
  116.0 2.8 %final.1 = (f32[4,4,64,128]{3,2,1,0:T(8,128)}, f32[4,4,64,128]{3,2,1,0:T(8,128)}) custom-call(s32[3]{0:T(128)} %pad_add_fusion.facts, f32[4,4,64,128]{3,2,1,0:T(8,128)} %base.1, f32[4,4,64,128]{3,2,1,0:T(8,128)} %state.3, f32[4,4,64,128]{3,2,1,0:T(8,128)} %get-tuple-element.4.spatial, f32[4,64,128]{2,1,0:T(8,128)} %get-tuple-element.5.step, ...), custom_call_target="tpu_custom_call" | custom-call | flops 1048576 | bytes 4194304 | tf_op jit(solution)/shard_map/final/pallas_call | solution.py:288
  (63 shorter events, 7.5 us)
Async XLA Ops:
  1.5 37.2 %collective-permute-start.4 = (f32[4,4,128]{2,1,0:T(4,128)S(1)}, f32[4,4,128]{2,1,0:T(4,128)S(1)}, u32[]{:S(2)}, u32[]{:S(2)}) collective-permute-start(f32[4,4,128]{2,1,0:T(4,128)S(1)} %bitcast.378), channel_id=1, source_target_pairs={{64,0},{128,64},{192,128},{256,192},{320,256},{384,320},{448,384},... | collective-permute-start | bytes 24584 | tf_op jit(solution)/shard_map/ppermute | solution.py:235
  3.5 35.3 %collective-permute-start.3 = (f32[4,4,128]{2,1,0:T(4,128)S(1)}, f32[4,4,128]{2,1,0:T(4,128)S(1)}, u32[]{:S(2)}, u32[]{:S(2)}) collective-permute-start(f32[4,4,128]{2,1,0:T(4,128)S(1)} %bitcast.377), channel_id=1, source_target_pairs={{0,64},{64,128},{128,192},{192,256},{256,320},{320,384},{384,448},... | collective-permute-start | bytes 24584 | tf_op jit(solution)/shard_map/ppermute | solution.py:234
  8.9 21.3 %copy-start = (f32[4,4,64,128]{3,2,1,0:T(8,128)S(1)}, f32[4,4,64,128]{3,2,1,0:T(8,128)}, u32[]{:S(2)}) copy-start(f32[4,4,64,128]{3,2,1,0:T(8,128)} %state.3) | copy-start | bytes 1572868
  8.9 44.6 %all-to-all-start = ((f32[8,128,128]{2,1,0:T(8,128)}), f32[8,128,128]{2,1,0:T(8,128)S(1)}, u32[]{:S(2)}, u32[]{:S(2)}) async-start(f32[8,128,128]{2,1,0:T(8,128)} %bitcast.23), calls=%async_computation | async-start | bytes 1048576 | tf_op jit(solution)/shard_map/all_to_all | solution.py:20
  15.7 37.1 %collective-permute-start.2 = (f32[8,64,128]{2,1,0:T(8,128)S(1)}, f32[8,64,128]{2,1,0:T(8,128)S(1)}, u32[]{:S(2)}, u32[]{:S(2)}) collective-permute-start(f32[8,64,128]{2,1,0:T(8,128)S(1)} %slice.174), channel_id=1, source_target_pairs={{0,8},{4,12},{8,0},{12,4},{16,24},{20,28},{24,16},{28,20},{32,40},... | collective-permute-start | bytes 786440 | tf_op jit(solution)/shard_map/ppermute | solution.py:228
  30.6 41.9 %collective-permute-start.1 = (f32[4,4,64]{2,1,0:T(4,128)S(1)}, f32[4,4,64]{2,1,0:T(4,128)S(1)}, u32[]{:S(2)}, u32[]{:S(2)}) collective-permute-start(f32[4,4,64]{2,1,0:T(4,128)S(1)} %bitcast.375), channel_id=1, source_target_pairs={{1,0},{2,1},{3,2},{0,3},{5,4},{6,5},{7,6},{4,7},{9,8},{10,9},{11,1... | collective-permute-start | bytes 12296 | tf_op jit(solution)/shard_map/ppermute | solution.py:255
  33.0 52.0 %collective-permute-start = (f32[4,4,64]{2,1,0:T(4,128)S(1)}, f32[4,4,64]{2,1,0:T(4,128)S(1)}, u32[]{:S(2)}, u32[]{:S(2)}) collective-permute-start(f32[4,4,64]{2,1,0:T(4,128)S(1)} %bitcast.374), channel_id=1, source_target_pairs={{0,1},{1,2},{2,3},{3,0},{4,5},{5,6},{6,7},{7,4},{8,9},{9,10},{10,1... | collective-permute-start | bytes 12296 | tf_op jit(solution)/shard_map/ppermute | solution.py:254
  36.2 0.7 copy-start.7
  36.5 0.7 copy-start.6
  37.3 0.8 copy-start.5
  38.8 14.0 %collective-permute-start.5 = (f32[8,4,128]{2,1,0:T(4,128)S(1)}, f32[8,4,128]{2,1,0:T(4,128)S(1)}, u32[]{:S(2)}, u32[]{:S(2)}) collective-permute-start(f32[8,4,128]{2,1,0:T(4,128)S(1)} %bitcast.368), channel_id=1, source_target_pairs={{64,72},{68,76},{72,64},{76,68},{80,88},{84,92},{88,80},{92,84},{9... | collective-permute-start | bytes 49160 | tf_op jit(solution)/shard_map/ppermute | solution.py:237
  53.5 10.6 %copy-start.1 = (f32[8,128,128]{2,1,0:T(8,128)}, f32[8,128,128]{2,1,0:T(8,128)S(1)}, u32[]{:S(2)}) copy-start(f32[8,128,128]{2,1,0:T(8,128)S(1)} %all-to-all-done.source) | copy-start | bytes 1572868
  53.5 14.2 %all-to-all-start.1 = ((f32[8,72,128]{2,1,0:T(8,128)}), f32[8,72,128]{2,1,0:T(8,128)S(1)}, u32[]{:S(2)}, u32[]{:S(2)}) async-start(f32[8,72,128]{2,1,0:T(8,128)} %pad_maximum_fusion), calls=%async_computation.1 | async-start | bytes 589824 | tf_op jit(solution)/shard_map/all_to_all | solution.py:20
  67.7 4.9 %copy-start.3 = (f32[8,72,128]{2,1,0:T(8,128)}, f32[8,72,128]{2,1,0:T(8,128)S(1)}, u32[]{:S(2)}) copy-start(f32[8,72,128]{2,1,0:T(8,128)S(1)} %all-to-all-done.1.source) | copy-start | bytes 884740
  67.7 12.4 %all-to-all-start.3 = ((f32[8,64,128]{2,1,0:T(8,128)}), f32[8,64,128]{2,1,0:T(8,128)S(1)}, u32[]{:S(2)}, u32[]{:S(2)}) async-start(f32[8,64,128]{2,1,0:T(8,128)} %outgoing.1), calls=%async_computation.3 | async-start | bytes 524288 | tf_op jit(solution)/shard_map/all_to_all | solution.py:20
  80.2 34.9 %all-to-all-start.2 = ((f32[8,136,128]{2,1,0:T(8,128)}), f32[8,136,128]{2,1,0:T(8,128)S(1)}, u32[]{:S(2)}, u32[]{:S(2)}) async-start(f32[8,136,128]{2,1,0:T(8,128)} %arrived.1), calls=%async_computation.2 | async-start | bytes 1114112 | tf_op jit(solution)/shard_map/all_to_all | solution.py:20
  85.0 30.0 %collective-permute-start.6 = (f32[8,64,128]{2,1,0:T(8,128)S(1)}, f32[8,64,128]{2,1,0:T(8,128)S(1)}, u32[]{:S(2)}, u32[]{:S(2)}) collective-permute-start(f32[8,64,128]{2,1,0:T(8,128)S(1)} %all-to-all-done.3), channel_id=1, source_target_pairs={{0,8},{4,12},{8,0},{12,4},{16,24},{20,28},{24,16},{28,20},{32,40},... | collective-permute-start | bytes 786440 | tf_op jit(solution)/shard_map/ppermute | solution.py:245
  115.1 0.7 copy-start.4
  115.1 0.9 copy-start.2

commit v2 on v1

v2 whole, which is shorter than its diff:
```python
import jax
import jax.numpy as jnp
from jax import lax
from jax.experimental import pallas as pl
from jax.experimental.pallas import tpu as pltpu
from jax.sharding import PartitionSpec as P

heat_ratio = 1.4
courant = 0.8
segment_coeff = 0.5

GROUPS = [[y * 4 + half * 2 + c for y in range(4) for c in range(2)] for half in range(2)]
PARTNER = [(i, i ^ 2) for i in range(16)]
VMEM = pl.BlockSpec(memory_space=pltpu.VMEM)
SMEM = pl.BlockSpec(memory_space=pltpu.SMEM)


def swap_members(value):
    return lax.all_to_all(value, "inst", 0, 0, tiled=True, axis_index_groups=GROUPS)


def primitives(dens, mom_norm, mom_tang, energy):
    inverse = 1.0 / dens
    norm = mom_norm * inverse
    tang = mom_tang * inverse
    pres = (heat_ratio - 1.0) * (energy - 0.5 * (mom_norm * norm + mom_tang * tang))
    enth = (energy + pres) * inverse
    return (dens, norm, tang, pres, enth, jnp.sqrt(dens), mom_norm)


def roe(left, right):
    dens_l, norm_l, tang_l, pres_l, enth_l, root_l, mass_l = left
    dens_r, norm_r, tang_r, pres_r, enth_r, root_r, mass_r = right
    weight = 1.0 / (root_l + root_r)
    share_l = root_l * weight
    share_r = root_r * weight
    norm = share_l * norm_l + share_r * norm_r
    tang = share_l * tang_l + share_r * tang_r
    enth = share_l * enth_l + share_r * enth_r
    dens = root_l * root_r
    kinetic = 0.5 * (norm * norm + tang * tang)
    cel_sq = (heat_ratio - 1.0) * (enth - kinetic)
    cel = jnp.sqrt(cel_sq)
    inverse = 1.0 / cel_sq
    jump_pres = pres_r - pres_l
    push = dens * cel * (norm_r - norm_l)
    half_inverse = 0.5 * inverse
    one = jnp.abs(norm - cel) * ((jump_pres - push) * half_inverse)
    four = jnp.abs(norm + cel) * ((jump_pres + push) * half_inverse)
    speed = jnp.abs(norm)
    two = speed * ((dens_r - dens_l) - jump_pres * inverse)
    three = speed * (dens * (tang_r - tang_l))
    outer = one + four
    acoustic = outer + two
    spread = cel * (four - one)
    flux_mass = 0.5 * (mass_l + mass_r - acoustic)
    flux_norm = 0.5 * (mass_l * norm_l + pres_l + mass_r * norm_r + pres_r - (acoustic * norm + spread))
    flux_tang = 0.5 * (mass_l * tang_l + mass_r * tang_r - (acoustic * tang + three))
    flux_energy = 0.5 * (
        mass_l * enth_l + mass_r * enth_r - (outer * enth + norm * spread + two * kinetic + three * tang)
    )
    return flux_mass, flux_norm, flux_tang, flux_energy


def place():
    inst = lax.axis_index("inst")
    return lax.axis_index("row"), inst, lax.rem(inst // 2, 2), (inst // 4) * 2 + lax.rem(inst, 2)


def place():
    inst = lax.axis_index("inst")
    return lax.axis_index("row"), inst, lax.rem(inst // 2, 2), (inst // 4) * 2 + lax.rem(inst, 2)


def wide_rows(ref, offset, stride, count=32):
    return jnp.concatenate([ref[pl.ds(offset + r, count, stride=stride), :] for r in range(8)], axis=1)


def parts(value):
    high = value.astype(jnp.bfloat16)
    return high, (value - high.astype(jnp.float32)).astype(jnp.bfloat16)


def half_rows(matrix, half):
    return jnp.concatenate(
        [matrix[pl.ds(pl.multiple_of(y * 16 + half * 8, 8), 8), :] for y in range(4)], axis=0
    )


def left_factor(rows, source_half):
    slot = lax.broadcasted_iota(jnp.int32, (64, 96), 0)
    column = lax.broadcasted_iota(jnp.int32, (64, 96), 1)
    place_in = lax.rem(column, 32)
    picked = slot == (place_in // 8) * 16 + source_half * 8 + lax.rem(place_in, 8)
    middle = (column >= 32) & (column < 64)
    zero, one = jnp.zeros((64, 96), jnp.float32), jnp.ones((64, 96), jnp.float32)
    pick_high = jnp.where(picked, jnp.where(middle, zero, one), zero).astype(jnp.bfloat16)
    pick_low = jnp.where(picked, jnp.where(middle, one, zero), zero).astype(jnp.bfloat16)
    high, low = parts(rows)
    both = jnp.dot(high, pick_high, preferred_element_type=jnp.float32) + jnp.dot(
        low, pick_low, preferred_element_type=jnp.float32
    )
    return both.astype(jnp.bfloat16)


def right_factor(value):
    high, low = parts(value)
    return jnp.concatenate([high, high, low], axis=0)


def split_kernel(state, octets, edges):
    for o in range(8):
        for i in range(4):
            for v in range(4):
                row = o * 128 + i * 32 + v * 8
                octets[row : row + 8, :] = state[v, i, 8 * o : 8 * o + 8, :]
    for v in range(4):
        edges[0, v] = state[v, :, 0, :]
        edges[1, v] = state[v, :, 63, :]


def outgoing_kernel(matrix, source, out):
    _, _, half, _ = place()
    lefts = [left_factor(half_rows(matrix, target_half), half) for target_half in (half, 1 - half)]
    for v in range(2):
        right = right_factor(wide_rows(source, (2 + v) * 8, 32))
        for k in range(2):
            total = jnp.dot(lefts[k], right, preferred_element_type=jnp.float32)
            for r in range(8):
                out[pl.ds(k * 16 + v * 8 + r, 32, stride=32), :] = total[:, r * 128 : r * 128 + 128]


def second_kernel(raw, up, down, partner, out):
    section, _, _, _ = place()
    from_above = (section == 2) | (section == 6)
    for o in range(8):
        v, own = o // 2, (up if o % 2 == 0 else down)
        mine = own[v]
        other = jnp.where(from_above if o % 2 == 0 else jnp.logical_not(from_above), partner[v], 0.0)
        for i in range(4):
            row = o * 72 + i * 18
            for p in range(2):
                out[row + p * 8 : row + p * 8 + 8, :] = raw[p, i, 8 * o : 8 * o + 8, :]
            out[row + 16 : row + 18, :] = jnp.concatenate([mine[i : i + 1], other[i : i + 1]], axis=0)


def arrived_kernel(matrix, resample, mixed, source, out):
    _, _, half, _ = place()
    rows = half_rows(matrix, half)
    own_left = left_factor(rows, half)
    other_left = left_factor(rows, 1 - half)
    for v in range(2):
        total = jnp.dot(own_left, right_factor(wide_rows(mixed, v * 8, 32)), preferred_element_type=jnp.float32)
        total = total + jnp.dot(
            other_left, right_factor(wide_rows(source, v * 8, 18)), preferred_element_type=jnp.float32
        )
        for r in range(8):
            out[pl.ds(v * 8 + r, 32, stride=18), :] = total[:, r * 128 : r * 128 + 128]
    weights = half_rows(resample, half)
    ghost = jnp.zeros((32, 128), jnp.float32)
    for k, source_half in enumerate((half, 1 - half)):
        edge = source[pl.ds(16 + k, 32, stride=18), :]
        ghost = ghost + jnp.dot(
            left_factor(weights, source_half), right_factor(edge), preferred_element_type=jnp.float32
        )
    for k in range(2):
        out[pl.ds(16 + k, 32, stride=18), :] = ghost


def spatial_kernel(state, first_column, last_column, from_left, from_right, out, step, prims, columns):
    lane = lax.broadcasted_iota(jnp.int32, (8, 128), 1)
    row = lax.broadcasted_iota(jnp.int32, (8, 128), 0)
    slot = pl.program_id(0)

    @pl.when(slot == 0)
    def _():
        faces = []
        for left, right in ((from_left, first_column), (last_column, from_right)):
            mass, tang, norm, energy = roe(
                primitives(*[left[v] for v in (0, 2, 1, 3)]), primitives(*[right[v] for v in (0, 2, 1, 3)])
            )
            faces.append((mass, norm, tang, energy))
        for i in range(4):
            rows = [faces[side][v][i : i + 1, :] for v in range(4) for side in range(2)]
            block = jnp.concatenate(rows, axis=0)
            columns[i] = jnp.concatenate([block, jnp.zeros((8, 64), jnp.float32)], axis=1).T

    for o in range(8):
        at = slice(8 * o, 8 * o + 8)
        cells = [state[v, 0, at, :] for v in range(4)]
        dens, norm, tang, pres, enth, root, _ = primitives(*cells)
        cel = jnp.sqrt(heat_ratio * pres / dens)
        step[0, at, :] = (segment_coeff * courant) / (jnp.abs(norm) + jnp.abs(tang) + 2.0 * cel)
        for k, value in enumerate((dens, norm, tang, pres, enth, root, cells[1], cells[2])):
            prims[k, at, :] = value
    previous = None
    for o in range(8):
        at = slice(8 * o, 8 * o + 8)
        here = [prims[k, at, :] for k in range(8)]
        if o < 7:
            below = [prims[k, 8 * o + 1 : 8 * o + 9, :] for k in range(8)]
        else:
            below = [pltpu.roll(x, 7, 0) for x in here]
        axial = roe(here[:7], below[:7])
        if o == 7:
            axial = [jnp.where(row == 7, 0.0, x) for x in axial]
        ahead = [pltpu.roll(x, 127, 1) for x in here]
        mass, tang, norm, energy = roe(
            [here[k] for k in (0, 2, 1, 3, 4, 5, 7)], [ahead[k] for k in (0, 2, 1, 3, 4, 5, 7)]
        )
        pitch = (mass, norm, tang, energy)
        shifted = [pltpu.roll(x, 1, 0) for x in axial]
        sides = columns[slot, at, :]
        for v in range(4):
            above = 0.0 if previous is None else jnp.broadcast_to(previous[v][0:1, :], (8, 128))
            net = axial[v] - jnp.where(row == 0, above, shifted[v])
            first = jnp.broadcast_to(sides[:, 2 * v : 2 * v + 1], (8, 128))
            last = jnp.broadcast_to(sides[:, 2 * v + 1 : 2 * v + 2], (8, 128))
            after = jnp.where(lane == 127, last, pitch[v])
            before = jnp.where(lane == 0, first, pltpu.roll(pitch[v], 1, 1))
            out[v, 0, at, :] = net + (after - before)
        previous = shifted


def final_kernel(base, edges, spatial, step, local, own, crossed, new_state, residual):
    section, inst, _, _ = place()
    active = jnp.where(section < 2, 45, jnp.where(section < 6, 64, 55))
    row = lax.broadcasted_iota(jnp.int32, (8, 128), 0)
    first_rows = [edges[0, v] for v in range(4)]
    last_rows = [edges[1, v] for v in range(4)]
    ghosts = [local[pl.ds(k * 72 + 16, 4, stride=18), :] for k in range(8)]
    up = [jnp.where(section == 0, first_rows[v], ghosts[2 * v]) for v in range(4)]
    down = [jnp.where(section == 7, last_rows[v], ghosts[2 * v + 1]) for v in range(4)]
    flux_up = roe(primitives(*up), primitives(*first_rows))
    flux_down = roe(primitives(*last_rows), primitives(*down))
    for i in range(4):
        live = inst * 4 + i < active
        for o in range(8):
            at = slice(8 * o, 8 * o + 8)
            factor = step[i, at, :]
            for v in range(4):
                total = spatial[v, i, at, :]
                if v < 2:
                    row_at = o * 72 + i * 18 + v * 8
                    total = total + local[row_at : row_at + 8, :]
                else:
                    rows = slice(v * 8 - 16, v * 8 - 8)
                    total = total + (own[o * 4 + i, rows, :] + crossed[o * 4 + i, rows, :])
                if o == 0:
                    edge = jnp.broadcast_to(flux_up[v][i : i + 1, :], (8, 128))
                    total = total - jnp.where(row == 0, edge, 0.0)
                if o == 7:
                    edge = jnp.broadcast_to(flux_down[v][i : i + 1, :], (8, 128))
                    total = total + jnp.where(row == 7, edge, 0.0)
                total = jnp.where(live, total, 0.0)
                residual[v, i, at, :] = total
                new_state[v, i, at, :] = base[v, i, at, :] - factor * total


def shape(*dims):
    return jax.ShapeDtypeStruct(dims, jnp.float32)


SMALL = pl.CostEstimate(flops=1000, bytes_accessed=1000, transcendentals=0)


def call(kernel, name, estimate, *operands, **options):
    return pl.pallas_call(kernel, name=name, cost_estimate=estimate, **options)(*operands)


def staged(needed, stage, *operands):
    given = jax.eval_shape(stage, *operands)
    return lax.cond(needed, stage, lambda *_: jax.tree.map(lambda x: jnp.zeros(x.shape, x.dtype), given), *operands)


def per_device(base_state, segment_state, spectral, donors, donor_weight):
    section, inst, _, member = place()
    matrix = spectral[0]
    needed = inst < 16

    def leave(state, matrix):
        arrived_half = lax.ppermute(state[:2], "inst", PARTNER)
        octets, edge_rows = call(
            split_kernel, "split", SMALL, state,
            out_shape=(shape(1024, 128), shape(2, 4, 4, 128)), in_specs=[VMEM], out_specs=(VMEM, VMEM),
        )
        mixed = swap_members(octets)
        from_up = lax.ppermute(edge_rows[1], "row", [(i, i + 1) for i in range(7)])
        from_down = lax.ppermute(edge_rows[0], "row", [(i + 1, i) for i in range(7)])
        meeting = [(1, 2), (2, 1), (5, 6), (6, 5)]
        partner_edges = lax.ppermute(
            jnp.where((section == 1) | (section == 5), edge_rows[1], edge_rows[0]),
            ("row", "inst"),
            [(r * 16 + a, s * 16 + b) for r, s in meeting for a, b in PARTNER],
        )
        outgoing = call(
            outgoing_kernel, "outgoing", SMALL, matrix, mixed,
            out_shape=shape(1024, 128), in_specs=[VMEM] * 2, out_specs=VMEM,
        )
        first_column = state[..., 0]
        last_column = state[..., 127]
        around = [(i, (i + 1) % 4) for i in range(4)]
        from_left = lax.ppermute(last_column, "cell", around)
        from_right = lax.ppermute(first_column, "cell", [(b, a) for a, b in around])
        returned = swap_members(outgoing).reshape(32, 32, 128)
        columns = (first_column, last_column, from_left, from_right)
        return arrived_half, mixed, returned, returned[:, 16:], edge_rows, from_up, from_down, partner_edges, columns

    arrived_half, mixed, returned, crossing, edge_rows, from_up, from_down, partner_edges, columns = staged(
        needed, leave, segment_state, matrix
    )
    crossed = lax.ppermute(crossing, "inst", PARTNER)

    side = lax.rem(member, 2)
    slots = jnp.arange(64, dtype=jnp.int32)
    donor = jnp.where(side == 0, donors[0, 0], donors[0, 1])
    weight = jnp.where(side == 0, donor_weight[0, 0], donor_weight[0, 1])[:, None]
    resample = (1.0 - weight) * (slots == donor[:, :1]).astype(jnp.float32) + weight * (
        slots == donor[:, 1:]
    ).astype(jnp.float32)

    def arrive(state, matrix, resample, mixed, raw, up, down, partner, columns):
        second = call(
            second_kernel, "second", SMALL, raw, up, down, partner,
            out_shape=shape(576, 128), in_specs=[VMEM] * 4, out_specs=VMEM,
        )
        totals = call(
            arrived_kernel, "arrived", SMALL, matrix, resample, mixed, swap_members(second),
            out_shape=shape(576, 128), in_specs=[VMEM] * 4, out_specs=VMEM,
        )
        slot_block = pl.BlockSpec((4, 1, 64, 128), lambda i: (0, i, 0, 0))
        spatial, step = call(
            spatial_kernel, "spatial", SMALL, state, *columns,
            grid=(4,),
            out_shape=(shape(4, 4, 64, 128), shape(4, 64, 128)),
            in_specs=[slot_block] + [pl.BlockSpec((4, 4, 64), lambda i: (0, 0, 0))] * 4,
            out_specs=(slot_block, pl.BlockSpec((1, 64, 128), lambda i: (i, 0, 0))),
            scratch_shapes=[pltpu.VMEM((8, 64, 128), jnp.float32), pltpu.VMEM((4, 128, 8), jnp.float32)],
        )
        return swap_members(totals), spatial, step

    local, spatial, step = staged(
        needed, arrive,
        segment_state, matrix, resample, mixed, arrived_half, from_up, from_down, partner_edges, columns,
    )
    whole = pl.BlockSpec((4, 4, 64, 128), lambda _: (0, 0, 0, 0))
    sums = pl.BlockSpec((32, 16, 128), lambda _: (0, 0, 0))
    return call(
        final_kernel, "final", SMALL, base_state, edge_rows, spatial, step, local, returned, crossed,
        grid=(1,),
        out_shape=(shape(4, 4, 64, 128), shape(4, 4, 64, 128)),
        in_specs=[
            whole, pl.BlockSpec((2, 4, 4, 128), lambda _: (0, 0, 0, 0)), whole,
            pl.BlockSpec((4, 64, 128), lambda _: (0, 0, 0)), pl.BlockSpec((576, 128), lambda _: (0, 0)), sums, sums,
        ],
        out_specs=(whole, whole),
    )


def solution(mesh):
    placed = (
        P(None, "inst", "row", "cell"),
        P(None, "inst", "row", "cell"),
        P("row", None, None),
        P("row", None, None, None),
        P("row", None, None),
    )
    return jax.shard_map(
        per_device,
        mesh=mesh,
        in_specs=placed,
        out_specs=(P(None, "inst", "row", "cell"), P(None, "inst", "row", "cell")),
        check_vma=False,
    )
```

time: 120 us -> 95.6 us (0.80)
  the two profiles are of different devices: /device:TPU:45 before, /device:TPU:32 now
where the time goes in v2:
time: 95.6 us; the launch traced here: 94.6 us
  starting transfers between devices  63.5 us (66%)
  waiting for transfers between devices  13.3 us (14%)
  Pallas kernels  12.3 us (13%)
  local copies, waits for them, and re-layouts  3.84 us (4%)
    all_to_all x4, starting transfers between devices, swap_members(): lax.all_to_all(value, 'inst', 0, 0, tiled=True, axis_index_groups=GROUPS)  18.2 us
    ppermute x1, starting transfers between devices, leave(): arrived_half = lax.ppermute(state[:2], 'inst', PARTNER)  14.8 us
    all_to_all x4, waiting for transfers between devices, swap_members(): lax.all_to_all(value, 'inst', 0, 0, tiled=True, axis_index_groups=GROUPS)  12.3 us
    pallas_call x6, Pallas kernels, call(): pl.pallas_call(kernel, name=name, cost_estimate=estimate, **options)  12.3 us
    ppermute x1, starting transfers between devices, leave(): lax.ppermute(jnp.where((section == 1) | (section == 5), edge_rows[1], edg...  9.19 us
    ppermute x1, starting transfers between devices, per_device(): crossed = lax.ppermute(crossing, 'inst', PARTNER)  8.2 us
    ppermute x1, starting transfers between devices, leave(): from_right = lax.ppermute(first_column, 'cell', [(b, a) for a, b in around])  3.65 us
    ppermute x1, starting transfers between devices, leave(): from_left = lax.ppermute(last_column, 'cell', around)  3.54 us
  transfers between devices with their start and end apart: 11, of which 3 were waited for; matrix products, arithmetic and copies ran while one was open for 2% of the time, Pallas kernels for 8%

profile of v2, /device:TPU:32, one launch (start us, length us, event | category | flops | bytes accessed | tf_op | source)
XLA Modules:
  0.0 94.6 jit_solution(7803570794402930588)
XLA Ops:
  0.6 52.6 %conditional.2 = (f32[2,4,64,128]{3,2,1,0:T(8,128)}, f32[1024,128]{1,0:T(8,128)S(1)}, f32[32,32,128]{2,1,0:T(8,128)}, f32[32,16,128]{2,1,0:T(8,128)S(1)}, f32[2,...) conditional(s32[]{:T(128)} %convert_element_type.2, () %tuple.36, ...), branch_computations={%region_0.1_spmd, %region_1.2_spmd} | conditional | flops 4051 | bytes 13052558 | solution.py:273
  0.6 1.9 %split.1 = (f32[1024,128]{1,0:T(8,128)}, f32[2,4,4,128]{3,2,1,0:T(4,128)S(1)}) custom-call(f32[4,4,64,128]{3,2,1,0:T(8,128)} %get-tuple-element.89.state), custom_call_target="tpu_custom_call" | custom-call | flops 1000 | bytes 1000 | tf_op jit(solution)/shard_map/cond/branch_1_fun/split/pallas_call | solution.py:268
  2.5 4.6 %all-to-all-start = ((f32[8,128,128]{2,1,0:T(8,128)}), f32[8,128,128]{2,1,0:T(8,128)S(1)}, u32[]{:S(2)}, u32[]{:S(2)}) async-start(f32[8,128,128]{2,1,0:T(8,128)} %bitcast.36), calls=%async_computation | async-start | bytes 1048576 | tf_op jit(solution)/shard_map/cond/branch_1_fun/all_to_all | solution.py:19
  7.2 14.8 %collective-permute-start = (f32[2,4,64,128]{3,2,1,0:T(8,128)S(1)}, f32[2,4,64,128]{3,2,1,0:T(8,128)}, u32[]{:S(2)}, u32[]{:S(2)}) collective-permute-start(f32[2,4,64,128]{3,2,1,0:T(8,128)S(1)} %slice.32), channel_id=1, source_target_pairs={{0,8},{4,12},{8,0},{12,4},{16,24},{20,28},{24,16},{28,20},{32,40},... | collective-permute-start | bytes 786440 | tf_op jit(solution)/shard_map/cond/branch_1_fun/ppermute | solution.py:282
  22.0 1.4 %outgoing.1 = f32[1024,128]{1,0:T(8,128)} custom-call(f32[64,64]{1,0:T(8,128)S(1)} %copy-done.9, f32[1024,128]{1,0:T(8,128)S(1)} %bitcast.30), custom_call_target="tpu_custom_call" | custom-call | flops 1000 | bytes 1000 | tf_op jit(solution)/shard_map/cond/branch_1_fun/outgoing/pallas_call | solution.py:268
  23.4 4.8 %all-to-all-start.1 = ((f32[8,128,128]{2,1,0:T(8,128)}), f32[8,128,128]{2,1,0:T(8,128)}, u32[]{:S(2)}, u32[]{:S(2)}) async-start(f32[8,128,128]{2,1,0:T(8,128)} %bitcast.32), calls=%async_computation.1 | async-start | bytes 1048576 | tf_op jit(solution)/shard_map/cond/branch_1_fun/all_to_all | solution.py:19
  28.2 2.9 %collective-permute-start.2 = (f32[4,4,128]{2,1,0:T(4,128)S(1)}, f32[4,4,128]{2,1,0:T(4,128)}, u32[]{:S(2)}, u32[]{:S(2)}) collective-permute-start(f32[4,4,128]{2,1,0:T(4,128)S(1)} %get-tuple-element.179), channel_id=1, source_target_pairs={{64,0},{128,64},{192,128},{256,192},{320,256},{384,320},{448,384},... | collective-permute-start | bytes 24584 | tf_op jit(solution)/shard_map/cond/branch_1_fun/ppermute | solution.py:289
  31.1 2.9 %collective-permute-start.1 = (f32[4,4,128]{2,1,0:T(4,128)S(1)}, f32[4,4,128]{2,1,0:T(4,128)}, u32[]{:S(2)}, u32[]{:S(2)}) collective-permute-start(f32[4,4,128]{2,1,0:T(4,128)S(1)} %get-tuple-element.180), channel_id=1, source_target_pairs={{0,64},{64,128},{128,192},{192,256},{256,320},{320,384},{384,448},... | collective-permute-start | bytes 24584 | tf_op jit(solution)/shard_map/cond/branch_1_fun/ppermute | solution.py:288
  34.7 3.5 %collective-permute-start.4 = (f32[4,4,64]{2,1,0:T(4,128)S(1)}, f32[4,4,64]{2,1,0:T(4,128)}, u32[]{:S(2)}, u32[]{:S(2)}) collective-permute-start(f32[4,4,64]{2,1,0:T(4,128)S(1)} %get-tuple-element.204), channel_id=1, source_target_pairs={{0,1},{1,2},{2,3},{3,0},{4,5},{5,6},{6,7},{7,4},{8,9},{9,10},{10,1... | collective-permute-start | bytes 12296 | tf_op jit(solution)/shard_map/cond/branch_1_fun/ppermute | solution.py:303
  38.3 9.2 %collective-permute-start.3 = (f32[4,4,128]{2,1,0:T(4,128)S(1)}, f32[4,4,128]{2,1,0:T(4,128)}, u32[]{:S(2)}, u32[]{:S(2)}) collective-permute-start(f32[4,4,128]{2,1,0:T(4,128)S(1)} %broadcast_select_fusion), channel_id=1, source_target_pairs={{64,136},{68,140},{72,128},{76,132},{80,152},{84,156},{88,144},{92... | collective-permute-start | bytes 24584 | tf_op jit(solution)/shard_map/cond/branch_1_fun/ppermute | solution.py:291
  47.5 3.6 %collective-permute-start.5 = (f32[4,4,64]{2,1,0:T(4,128)S(1)}, f32[4,4,64]{2,1,0:T(4,128)}, u32[]{:S(2)}, u32[]{:S(2)}) collective-permute-start(f32[4,4,64]{2,1,0:T(4,128)S(1)} %get-tuple-element.203), channel_id=1, source_target_pairs={{1,0},{2,1},{3,2},{0,3},{5,4},{6,5},{7,6},{4,7},{9,8},{10,9},{11,1... | collective-permute-start | bytes 12296 | tf_op jit(solution)/shard_map/cond/branch_1_fun/ppermute | solution.py:304
  51.2 1.0 %slice.44 = f32[32,16,128]{2,1,0:T(8,128)S(1)} slice(f32[32,32,128]{2,1,0:T(8,128)} %bitcast.3), slice={[0:32], [16:32], [0:128]} | slice | bytes 524288 | tf_op jit(solution)/shard_map/cond/branch_1_fun/slice | solution.py:307
  52.2 1.0 %collective-permute-done.5 = f32[4,4,64]{2,1,0:T(4,128)} collective-permute-done((f32[4,4,64]{2,1,0:T(4,128)S(1)}, f32[4,4,64]{2,1,0:T(4,128)}, u32[]{:S(2)}, u32[]{:S(2)}) %collective-permute-start.5) | collective-permute-done | bytes 4128 | tf_op jit(solution)/shard_map/cond/branch_1_fun/ppermute | solution.py:304
  53.3 8.2 %collective-permute-start.6 = (f32[32,16,128]{2,1,0:T(8,128)S(1)}, f32[32,16,128]{2,1,0:T(8,128)S(1)}, u32[]{:S(2)}, u32[]{:S(2)}) collective-permute-start(f32[32,16,128]{2,1,0:T(8,128)S(1)} %get-tuple-element.144), channel_id=1, source_target_pairs={{0,8},{4,12},{8,0},{12,4},{16,24},{20,28},{24,16},{28,20},{32,40},... | collective-permute-start | bytes 786440 | tf_op jit(solution)/shard_map/ppermute | solution.py:312
  61.5 0.7 copy-done.8
  62.2 29.3 %conditional.3 = (f32[576,128]{1,0:T(8,128)}, f32[4,4,64,128]{3,2,1,0:T(8,128)S(1)}, f32[4,64,128]{2,1,0:T(8,128)S(1)}) conditional(s32[]{:T(128)} %convert_element_type.2, () %tuple.38, (s32[]{:T(128)}, pred[]{:T(512)}, s32[1,2,64,2]{2,3,1,0:T(2,128)S(1)}, s32[64,64]{1,0:T(8,128)S(1)}, f32[1,2,64]{2,1,0:T(2,128)S(1)}, ...), branch_computations={%region_2.3_spmd, %region_3.4_spmd} | conditional | flops 23755 | bytes 5103370 | solution.py:273
  62.2 1.7 %second.1 = f32[576,128]{1,0:T(8,128)} custom-call(f32[2,4,64,128]{3,2,1,0:T(8,128)} %get-tuple-element.102.raw, f32[4,4,128]{2,1,0:T(4,128)} %get-tuple-element.103.up, f32[4,4,128]{2,1,0:T(4,128)} %get-tuple-element.104.down, f32[4,4,128]{2,1,0:T(4,128)} %get-tuple-element.105.partner), custom_call_target="tpu_custom_call" | custom-call | flops 1000 | bytes 1000 | tf_op jit(solution)/shard_map/cond/branch_1_fun/second/pallas_call | solution.py:268
  63.9 4.7 %all-to-all-start.2 = ((f32[8,72,128]{2,1,0:T(8,128)}), f32[8,72,128]{2,1,0:T(8,128)S(1)}, u32[]{:S(2)}, u32[]{:S(2)}) async-start(f32[8,72,128]{2,1,0:T(8,128)} %bitcast.33), calls=%async_computation.2 | async-start | bytes 589824 | tf_op jit(solution)/shard_map/cond/branch_1_fun/all_to_all | solution.py:19
  69.4 7.1 %all-to-all-done.2 = f32[8,72,128]{2,1,0:T(8,128)S(1)} async-done(((f32[8,72,128]{2,1,0:T(8,128)}), f32[8,72,128]{2,1,0:T(8,128)S(1)}, u32[]{:S(2)}, u32[]{:S(2)}) %all-to-all-start.2) | async-done | bytes 294944 | tf_op jit(solution)/shard_map/cond/branch_1_fun/all_to_all | solution.py:19
  77.2 2.2 %arrived.1 = f32[576,128]{1,0:T(8,128)} custom-call(f32[64,64]{1,0:T(8,128)S(1)} %get-tuple-element.94.matrix, f32[64,64]{1,0:T(8,128)} %select_add_fusion.resample, f32[1024,128]{1,0:T(8,128)S(1)} %get-tuple-element.101.mixed, f32[576,128]{1,0:T(8,128)} %bitcast.34), custom_call_target="tpu_custom_call" | custom-call | flops 1000 | bytes 1000 | tf_op jit(solution)/shard_map/cond/branch_1_fun/arrived/pallas_call | solution.py:268
  79.5 4.2 %all-to-all-start.3 = ((f32[8,72,128]{2,1,0:T(8,128)}), f32[8,72,128]{2,1,0:T(8,128)}, u32[]{:S(2)}, u32[]{:S(2)}) async-start(f32[8,72,128]{2,1,0:T(8,128)} %bitcast.35), calls=%async_computation.3 | async-start | bytes 589824 | tf_op jit(solution)/shard_map/cond/branch_1_fun/all_to_all | solution.py:19
  83.7 2.7 %spatial.1 = (f32[4,4,64,128]{3,2,1,0:T(8,128)S(1)}, f32[4,64,128]{2,1,0:T(8,128)S(1)}) custom-call(f32[4,4,64,128]{3,2,1,0:T(8,128)S(1)} %copy-done.1, f32[4,4,64]{2,1,0:T(4,128)S(1)} %get-tuple-element.107.first_column, f32[4,4,64]{2,1,0:T(4,128)S(1)} %get-tuple-element.108.last_column, f32[4,4,64]{2,1,0:T(4,128)} %get-tuple-element.109.from_left, ...), custom_call_target="tpu_custom_call" | custom-call | flops 1000 | bytes 1000 | tf_op jit(solution)/shard_map/cond/branch_1_fun/spatial/pallas_call | solution.py:268
  86.4 5.2 %all-to-all-done.3 = f32[8,72,128]{2,1,0:T(8,128)} async-done(((f32[8,72,128]{2,1,0:T(8,128)}), f32[8,72,128]{2,1,0:T(8,128)}, u32[]{:S(2)}, u32[]{:S(2)}) %all-to-all-start.3) | async-done | bytes 294944 | tf_op jit(solution)/shard_map/cond/branch_1_fun/all_to_all | solution.py:19
  92.3 2.4 %final.1 = (f32[4,4,64,128]{3,2,1,0:T(8,128)}, f32[4,4,64,128]{3,2,1,0:T(8,128)}) custom-call(f32[4,4,64,128]{3,2,1,0:T(8,128)} %base.1, f32[2,4,4,128]{3,2,1,0:T(4,128)S(1)} %get-tuple-element.130.edges, f32[4,4,64,128]{3,2,1,0:T(8,128)S(1)} %get-tuple-element.140.spatial, f32[4,64,128]{2,1,0:T(8,128)S(1)} %get-tuple-element.141.step, ...), custom_call_target="tpu_custom_call" | custom-call | flops 1000 | bytes 1000 | tf_op jit(solution)/shard_map/final/pallas_call | solution.py:268
  (49 shorter events, 2.9 us)
Async XLA Ops:
  2.5 35.8 %copy-start.5 = (f32[2,4,4,128]{3,2,1,0:T(4,128)}, f32[2,4,4,128]{3,2,1,0:T(4,128)S(1)}, u32[]{:S(2)}) copy-start(f32[2,4,4,128]{3,2,1,0:T(4,128)S(1)} %get-tuple-element.199) | copy-start | bytes 49156 | tf_op jit(solution)/shard_map/cond
  2.5 4.6 %copy-start = (f32[4,4,64,128]{3,2,1,0:T(8,128)S(1)}, f32[4,4,64,128]{3,2,1,0:T(8,128)}, u32[]{:S(2)}) copy-start(f32[4,4,64,128]{3,2,1,0:T(8,128)} %get-tuple-element.89.state) | copy-start | bytes 1572868 | tf_op jit(solution)/shard_map/cond
  2.5 19.5 %all-to-all-start = ((f32[8,128,128]{2,1,0:T(8,128)}), f32[8,128,128]{2,1,0:T(8,128)S(1)}, u32[]{:S(2)}, u32[]{:S(2)}) async-start(f32[8,128,128]{2,1,0:T(8,128)} %bitcast.36), calls=%async_computation | async-start | bytes 1048576 | tf_op jit(solution)/shard_map/cond/branch_1_fun/all_to_all | solution.py:19
  7.1 14.9 %copy-start.9 = (f32[64,64]{1,0:T(8,128)S(1)}, f32[64,64]{1,0:T(8,128)}, u32[]{:S(2)}) copy-start(f32[64,64]{1,0:T(8,128)} %get-tuple-element.91.matrix) | copy-start | bytes 49156 | tf_op jit(solution)/shard_map/cond
  7.2 46.0 %collective-permute-start = (f32[2,4,64,128]{3,2,1,0:T(8,128)S(1)}, f32[2,4,64,128]{3,2,1,0:T(8,128)}, u32[]{:S(2)}, u32[]{:S(2)}) collective-permute-start(f32[2,4,64,128]{3,2,1,0:T(8,128)S(1)} %slice.32), channel_id=1, source_target_pairs={{0,8},{4,12},{8,0},{12,4},{16,24},{20,28},{24,16},{28,20},{32,40},... | collective-permute-start | bytes 786440 | tf_op jit(solution)/shard_map/cond/branch_1_fun/ppermute | solution.py:282
  22.0 1.4 %copy-start.2 = (f32[8,128,128]{2,1,0:T(8,128)}, f32[8,128,128]{2,1,0:T(8,128)S(1)}, u32[]{:S(2)}) copy-start(f32[8,128,128]{2,1,0:T(8,128)S(1)} %all-to-all-done) | copy-start | bytes 1572868 | tf_op jit(solution)/shard_map/cond
  23.4 27.8 %all-to-all-start.1 = ((f32[8,128,128]{2,1,0:T(8,128)}), f32[8,128,128]{2,1,0:T(8,128)}, u32[]{:S(2)}, u32[]{:S(2)}) async-start(f32[8,128,128]{2,1,0:T(8,128)} %bitcast.32), calls=%async_computation.1 | async-start | bytes 1048576 | tf_op jit(solution)/shard_map/cond/branch_1_fun/all_to_all | solution.py:19
  28.2 25.0 %collective-permute-start.2 = (f32[4,4,128]{2,1,0:T(4,128)S(1)}, f32[4,4,128]{2,1,0:T(4,128)}, u32[]{:S(2)}, u32[]{:S(2)}) collective-permute-start(f32[4,4,128]{2,1,0:T(4,128)S(1)} %get-tuple-element.179), channel_id=1, source_target_pairs={{64,0},{128,64},{192,128},{256,192},{320,256},{384,320},{448,384},... | collective-permute-start | bytes 24584 | tf_op jit(solution)/shard_map/cond/branch_1_fun/ppermute | solution.py:289
  31.1 22.1 %collective-permute-start.1 = (f32[4,4,128]{2,1,0:T(4,128)S(1)}, f32[4,4,128]{2,1,0:T(4,128)}, u32[]{:S(2)}, u32[]{:S(2)}) collective-permute-start(f32[4,4,128]{2,1,0:T(4,128)S(1)} %get-tuple-element.180), channel_id=1, source_target_pairs={{0,64},{64,128},{128,192},{192,256},{256,320},{320,384},{384,448},... | collective-permute-start | bytes 24584 | tf_op jit(solution)/shard_map/cond/branch_1_fun/ppermute | solution.py:288
  34.7 18.5 %copy-start.3 = (f32[8,128,128]{2,1,0:T(8,128)S(1)}, f32[8,128,128]{2,1,0:T(8,128)}, u32[]{:S(2)}) copy-start(f32[8,128,128]{2,1,0:T(8,128)} %copy-done.2) | copy-start | bytes 1572868 | tf_op jit(solution)/shard_map/cond
  34.7 3.6 %copy-start.10 = (f32[4,4,64]{2,1,0:T(4,128)}, f32[4,4,64]{2,1,0:T(4,128)S(1)}, u32[]{:S(2)}) copy-start(f32[4,4,64]{2,1,0:T(4,128)S(1)} %get-tuple-element.204) | copy-start | bytes 12292 | tf_op jit(solution)/shard_map/cond
  34.7 12.8 %copy-start.12 = (f32[4,4,64]{2,1,0:T(4,128)}, f32[4,4,64]{2,1,0:T(4,128)S(1)}, u32[]{:S(2)}) copy-start(f32[4,4,64]{2,1,0:T(4,128)S(1)} %get-tuple-element.203) | copy-start | bytes 12292 | tf_op jit(solution)/shard_map/cond
  34.7 12.8 %collective-permute-start.4 = (f32[4,4,64]{2,1,0:T(4,128)S(1)}, f32[4,4,64]{2,1,0:T(4,128)}, u32[]{:S(2)}, u32[]{:S(2)}) collective-permute-start(f32[4,4,64]{2,1,0:T(4,128)S(1)} %get-tuple-element.204), channel_id=1, source_target_pairs={{0,1},{1,2},{2,3},{3,0},{4,5},{5,6},{6,7},{7,4},{8,9},{9,10},{10,1... | collective-permute-start | bytes 12296 | tf_op jit(solution)/shard_map/cond/branch_1_fun/ppermute | solution.py:303
  38.3 14.9 %collective-permute-start.3 = (f32[4,4,128]{2,1,0:T(4,128)S(1)}, f32[4,4,128]{2,1,0:T(4,128)}, u32[]{:S(2)}, u32[]{:S(2)}) collective-permute-start(f32[4,4,128]{2,1,0:T(4,128)S(1)} %broadcast_select_fusion), channel_id=1, source_target_pairs={{64,136},{68,140},{72,128},{76,132},{80,152},{84,156},{88,144},{92... | collective-permute-start | bytes 24584 | tf_op jit(solution)/shard_map/cond/branch_1_fun/ppermute | solution.py:291
  47.5 5.7 %collective-permute-start.5 = (f32[4,4,64]{2,1,0:T(4,128)S(1)}, f32[4,4,64]{2,1,0:T(4,128)}, u32[]{:S(2)}, u32[]{:S(2)}) collective-permute-start(f32[4,4,64]{2,1,0:T(4,128)S(1)} %get-tuple-element.203), channel_id=1, source_target_pairs={{1,0},{2,1},{3,2},{0,3},{5,4},{6,5},{7,6},{4,7},{9,8},{10,9},{11,1... | collective-permute-start | bytes 12296 | tf_op jit(solution)/shard_map/cond/branch_1_fun/ppermute | solution.py:304
  51.2 2.0 %copy-start.6 = (f32[2,4,4,128]{3,2,1,0:T(4,128)S(1)}, f32[2,4,4,128]{3,2,1,0:T(4,128)}, u32[]{:S(2)}) copy-start(f32[2,4,4,128]{3,2,1,0:T(4,128)} %copy-done.5) | copy-start | bytes 49156 | tf_op jit(solution)/shard_map/cond
  51.2 2.0 %copy-start.11 = (f32[4,4,64]{2,1,0:T(4,128)S(1)}, f32[4,4,64]{2,1,0:T(4,128)}, u32[]{:S(2)}) copy-start(f32[4,4,64]{2,1,0:T(4,128)} %copy-done.10) | copy-start | bytes 12292 | tf_op jit(solution)/shard_map/cond
  51.2 2.0 %copy-start.13 = (f32[4,4,64]{2,1,0:T(4,128)S(1)}, f32[4,4,64]{2,1,0:T(4,128)}, u32[]{:S(2)}) copy-start(f32[4,4,64]{2,1,0:T(4,128)} %copy-done.12) | copy-start | bytes 12292 | tf_op jit(solution)/shard_map/cond
  53.3 38.3 %collective-permute-start.6 = (f32[32,16,128]{2,1,0:T(8,128)S(1)}, f32[32,16,128]{2,1,0:T(8,128)S(1)}, u32[]{:S(2)}, u32[]{:S(2)}) collective-permute-start(f32[32,16,128]{2,1,0:T(8,128)S(1)} %get-tuple-element.144), channel_id=1, source_target_pairs={{0,8},{4,12},{8,0},{12,4},{16,24},{20,28},{24,16},{28,20},{32,40},... | collective-permute-start | bytes 786440 | tf_op jit(solution)/shard_map/ppermute | solution.py:312
  61.5 0.8 copy-start.8
  61.5 0.7 copy-start.14
  63.9 12.6 %all-to-all-start.2 = ((f32[8,72,128]{2,1,0:T(8,128)}), f32[8,72,128]{2,1,0:T(8,128)S(1)}, u32[]{:S(2)}, u32[]{:S(2)}) async-start(f32[8,72,128]{2,1,0:T(8,128)} %bitcast.33), calls=%async_computation.2 | async-start | bytes 589824 | tf_op jit(solution)/shard_map/cond/branch_1_fun/all_to_all | solution.py:19
  79.5 4.2 %copy-start.1 = (f32[4,4,64,128]{3,2,1,0:T(8,128)S(1)}, f32[4,4,64,128]{3,2,1,0:T(8,128)}, u32[]{:S(2)}) copy-start(f32[4,4,64,128]{3,2,1,0:T(8,128)} %get-tuple-element.106.state) | copy-start | bytes 1572868 | tf_op jit(solution)/shard_map/cond
  79.5 12.1 %all-to-all-start.3 = ((f32[8,72,128]{2,1,0:T(8,128)}), f32[8,72,128]{2,1,0:T(8,128)}, u32[]{:S(2)}, u32[]{:S(2)}) async-start(f32[8,72,128]{2,1,0:T(8,128)} %bitcast.35), calls=%async_computation.3 | async-start | bytes 589824 | tf_op jit(solution)/shard_map/cond/branch_1_fun/all_to_all | solution.py:19
  (3 other events, 2.2 us)

commit v3 on v2

--- a/solution.py
+++ b/solution.py
@@ -119,52 +119,54 @@
         edges[1, v] = state[v, :, 63, :]
 
 
-def outgoing_kernel(matrix, source, out):
-    _, _, half, _ = place()
-    lefts = [left_factor(half_rows(matrix, target_half), half) for target_half in (half, 1 - half)]
+def pack_half_kernel(mixed, *rest):
+    out = rest[-1]
+    for k in range(32):
+        out[k * 16 : k * 16 + 16, :] = mixed[k * 32 : k * 32 + 16, :]
+
+
+def outgoing_kernel(matrix, source, up, down, partner, out):
+    section, _, half, _ = place()
+    from_above = (section == 2) | (section == 6)
+    left = left_factor(half_rows(matrix, 1 - half), half)
     for v in range(2):
-        right = right_factor(wide_rows(source, (2 + v) * 8, 32))
-        for k in range(2):
-            total = jnp.dot(lefts[k], right, preferred_element_type=jnp.float32)
-            for r in range(8):
-                out[pl.ds(k * 16 + v * 8 + r, 32, stride=32), :] = total[:, r * 128 : r * 128 + 128]
-
-
-def second_kernel(raw, up, down, partner, out):
-    section, _, _, _ = place()
-    from_above = (section == 2) | (section == 6)
-    for o in range(8):
-        v, own = o // 2, (up if o % 2 == 0 else down)
-        mine = own[v]
-        other = jnp.where(from_above if o % 2 == 0 else jnp.logical_not(from_above), partner[v], 0.0)
+        total = jnp.dot(left, right_factor(wide_rows(source, (2 + v) * 8, 32)), preferred_element_type=jnp.float32)
+        for r in range(8):
+            out[pl.ds(v * 8 + r, 32, stride=18), :] = total[:, r * 128 : r * 128 + 128]
+    for m in range(8):
+        mine = (up if m % 2 == 0 else down)[m // 2]
+        other = jnp.where(from_above if m % 2 == 0 else jnp.logical_not(from_above), partner[m // 2], 0.0)
         for i in range(4):
-            row = o * 72 + i * 18
-            for p in range(2):
-                out[row + p * 8 : row + p * 8 + 8, :] = raw[p, i, 8 * o : 8 * o + 8, :]
-            out[row + 16 : row + 18, :] = jnp.concatenate([mine[i : i + 1], other[i : i + 1]], axis=0)
-
-
-def arrived_kernel(matrix, resample, mixed, source, out):
+            row = (m * 4 + i) * 18 + 16
+            out[row : row + 2, :] = jnp.concatenate([mine[i : i + 1], other[i : i + 1]], axis=0)
+
+
+def pack_kernel(returned, *rest):
+    out = rest[-1]
+    for k in range(32):
+        out[k * 16 : k * 16 + 16, :] = returned[k * 18 : k * 18 + 16, :]
+
+
+def arrived_kernel(matrix, resample, mixed, returned, source, out):
     _, _, half, _ = place()
     rows = half_rows(matrix, half)
     own_left = left_factor(rows, half)
     other_left = left_factor(rows, 1 - half)
-    for v in range(2):
+    for v in range(4):
         total = jnp.dot(own_left, right_factor(wide_rows(mixed, v * 8, 32)), preferred_element_type=jnp.float32)
-        total = total + jnp.dot(
-            other_left, right_factor(wide_rows(source, v * 8, 18)), preferred_element_type=jnp.float32
-        )
+        if v < 2:
+            total = total + jnp.dot(
+                other_left, right_factor(wide_rows(source, v * 8, 16)), preferred_element_type=jnp.float32
+            )
         for r in range(8):
-            out[pl.ds(v * 8 + r, 32, stride=18), :] = total[:, r * 128 : r * 128 + 128]
+            out[pl.ds(v * 8 + r, 32, stride=34), :] = total[:, r * 128 : r * 128 + 128]
     weights = half_rows(resample, half)
     ghost = jnp.zeros((32, 128), jnp.float32)
     for k, source_half in enumerate((half, 1 - half)):
-        edge = source[pl.ds(16 + k, 32, stride=18), :]
-        ghost = ghost + jnp.dot(
-            left_factor(weights, source_half), right_factor(edge), preferred_element_type=jnp.float32
-        )
+        edge = right_factor(returned[pl.ds(16 + k, 32, stride=18), :])
+        ghost = ghost + jnp.dot(left_factor(weights, source_half), edge, preferred_element_type=jnp.float32)
     for k in range(2):
-        out[pl.ds(16 + k, 32, stride=18), :] = ghost
+        out[pl.ds(32 + k, 32, stride=34), :] = ghost
 
 
 def spatial_kernel(state, first_column, last_column, from_left, from_right, out, step, prims, columns):
@@ -222,13 +224,13 @@
         previous = shifted
 
 
-def final_kernel(base, edges, spatial, step, local, own, crossed, new_state, residual):
+def final_kernel(base, edges, spatial, step, local, crossed, new_state, residual):
     section, inst, _, _ = place()
     active = jnp.where(section < 2, 45, jnp.where(section < 6, 64, 55))
     row = lax.broadcasted_iota(jnp.int32, (8, 128), 0)
     first_rows = [edges[0, v] for v in range(4)]
     last_rows = [edges[1, v] for v in range(4)]
-    ghosts = [local[pl.ds(k * 72 + 16, 4, stride=18), :] for k in range(8)]
+    ghosts = [local[pl.ds(k * 136 + 32, 4, stride=34), :] for k in range(8)]
     up = [jnp.where(section == 0, first_rows[v], ghosts[2 * v]) for v in range(4)]
     down = [jnp.where(section == 7, last_rows[v], ghosts[2 * v + 1]) for v in range(4)]
     flux_up = roe(primitives(*up), primitives(*first_rows))
@@ -239,13 +241,10 @@
             at = slice(8 * o, 8 * o + 8)
             factor = step[i, at, :]
             for v in range(4):
-                total = spatial[v, i, at, :]
-                if v < 2:
-                    row_at = o * 72 + i * 18 + v * 8
-                    total = total + local[row_at : row_at + 8, :]
-                else:
-                    rows = slice(v * 8 - 16, v * 8 - 8)
-                    total = total + (own[o * 4 + i, rows, :] + crossed[o * 4 + i, rows, :])
+                local_at, crossed_at = (o * 4 + i) * 34 + v * 8, (o * 4 + i) * 16 + v * 8 - 16
+                total = spatial[v, i, at, :] + local[local_at : local_at + 8, :]
+                if v >= 2:
+                    total = total + crossed[crossed_at : crossed_at + 8, :]
                 if o == 0:
                     edge = jnp.broadcast_to(flux_up[v][i : i + 1, :], (8, 128))
                     total = total - jnp.where(row == 0, edge, 0.0)
@@ -277,37 +276,40 @@
     section, inst, _, member = place()
     matrix = spectral[0]
     needed = inst < 16
-
-    def leave(state, matrix):
-        arrived_half = lax.ppermute(state[:2], "inst", PARTNER)
-        octets, edge_rows = call(
-            split_kernel, "split", SMALL, state,
-            out_shape=(shape(1024, 128), shape(2, 4, 4, 128)), in_specs=[VMEM], out_specs=(VMEM, VMEM),
-        )
-        mixed = swap_members(octets)
-        from_up = lax.ppermute(edge_rows[1], "row", [(i, i + 1) for i in range(7)])
-        from_down = lax.ppermute(edge_rows[0], "row", [(i + 1, i) for i in range(7)])
-        meeting = [(1, 2), (2, 1), (5, 6), (6, 5)]
-        partner_edges = lax.ppermute(
-            jnp.where((section == 1) | (section == 5), edge_rows[1], edge_rows[0]),
-            ("row", "inst"),
-            [(r * 16 + a, s * 16 + b) for r, s in meeting for a, b in PARTNER],
-        )
+    anywhere = pl.BlockSpec(memory_space=pl.ANY)
+
+    octets, edge_rows = call(
+        split_kernel, "split", SMALL, segment_state,
+        out_shape=(shape(1024, 128), shape(2, 4, 4, 128)), in_specs=[VMEM], out_specs=(VMEM, VMEM),
+    )
+    mixed = swap_members(octets)
+    from_up = lax.ppermute(edge_rows[1], "row", [(i, i + 1) for i in range(7)])
+    from_down = lax.ppermute(edge_rows[0], "row", [(i + 1, i) for i in range(7)])
+    meeting = [(1, 2), (2, 1), (5, 6), (6, 5)]
+    partner_edges = lax.ppermute(
+        jnp.where((section == 1) | (section == 5), edge_rows[1], edge_rows[0]),
+        ("row", "inst"),
+        [(r * 16 + a, s * 16 + b) for r, s in meeting for a, b in PARTNER],
+    )
+    half = call(
+        pack_half_kernel, "half", SMALL, mixed,
+        out_shape=shape(512, 128), in_specs=[VMEM], out_specs=VMEM,
+    )
+    arrived_half = lax.ppermute(half, "inst", PARTNER)
+
+    def leave(matrix, mixed, up, down, partner):
         outgoing = call(
-            outgoing_kernel, "outgoing", SMALL, matrix, mixed,
-            out_shape=shape(1024, 128), in_specs=[VMEM] * 2, out_specs=VMEM,
-        )
-        first_column = state[..., 0]
-        last_column = state[..., 127]
-        around = [(i, (i + 1) % 4) for i in range(4)]
-        from_left = lax.ppermute(last_column, "cell", around)
-        from_right = lax.ppermute(first_column, "cell", [(b, a) for a, b in around])
-        returned = swap_members(outgoing).reshape(32, 32, 128)
-        columns = (first_column, last_column, from_left, from_right)
-        return arrived_half, mixed, returned, returned[:, 16:], edge_rows, from_up, from_down, partner_edges, columns
-
-    arrived_half, mixed, returned, crossing, edge_rows, from_up, from_down, partner_edges, columns = staged(
-        needed, leave, segment_state, matrix
+            outgoing_kernel, "outgoing", SMALL, matrix, mixed, up, down, partner,
+            out_shape=shape(576, 128), in_specs=[VMEM] * 5, out_specs=VMEM,
+        )
+        returned = swap_members(outgoing)
+        crossing = call(
+            pack_kernel, "pack", SMALL, returned, out_shape=shape(512, 128), in_specs=[VMEM], out_specs=VMEM,
+        )
+        return returned, crossing
+
+    returned, crossing = staged(
+        needed, leave, matrix, mixed, from_up, from_down, partner_edges
     )
     crossed = lax.ppermute(crossing, "inst", PARTNER)
 
@@ -319,18 +321,19 @@
         slots == donor[:, 1:]
     ).astype(jnp.float32)
 
-    def arrive(state, matrix, resample, mixed, raw, up, down, partner, columns):
-        second = call(
-            second_kernel, "second", SMALL, raw, up, down, partner,
-            out_shape=shape(576, 128), in_specs=[VMEM] * 4, out_specs=VMEM,
-        )
+    def arrive(state, matrix, resample, mixed, returned, arrived_half):
+        first_column = state[..., 0]
+        last_column = state[..., 127]
+        around = [(i, (i + 1) % 4) for i in range(4)]
+        from_left = lax.ppermute(last_column, "cell", around)
+        from_right = lax.ppermute(first_column, "cell", [(b, a) for a, b in around])
         totals = call(
-            arrived_kernel, "arrived", SMALL, matrix, resample, mixed, swap_members(second),
-            out_shape=shape(576, 128), in_specs=[VMEM] * 4, out_specs=VMEM,
+            arrived_kernel, "arrived", SMALL, matrix, resample, mixed, returned, arrived_half,
+            out_shape=shape(1088, 128), in_specs=[VMEM] * 5, out_specs=VMEM,
         )
         slot_block = pl.BlockSpec((4, 1, 64, 128), lambda i: (0, i, 0, 0))
         spatial, step = call(
-            spatial_kernel, "spatial", SMALL, state, *columns,
+            spatial_kernel, "spatial", SMALL, state, first_column, last_column, from_left, from_right,
             grid=(4,),
             out_shape=(shape(4, 4, 64, 128), shape(4, 64, 128)),
             in_specs=[slot_block] + [pl.BlockSpec((4, 4, 64), lambda i: (0, 0, 0))] * 4,
@@ -340,20 +343,13 @@
         return swap_members(totals), spatial, step
 
     local, spatial, step = staged(
-        needed, arrive,
-        segment_state, matrix, resample, mixed, arrived_half, from_up, from_down, partner_edges, columns,
-    )
-    whole = pl.BlockSpec((4, 4, 64, 128), lambda _: (0, 0, 0, 0))
-    sums = pl.BlockSpec((32, 16, 128), lambda _: (0, 0, 0))
+        needed, arrive, segment_state, matrix, resample, mixed, returned, arrived_half
+    )
     return call(
-        final_kernel, "final", SMALL, base_state, edge_rows, spatial, step, local, returned, crossed,
-        grid=(1,),
+        final_kernel, "final", SMALL, base_state, edge_rows, spatial, step, local, crossed,
         out_shape=(shape(4, 4, 64, 128), shape(4, 4, 64, 128)),
-        in_specs=[
-            whole, pl.BlockSpec((2, 4, 4, 128), lambda _: (0, 0, 0, 0)), whole,
-            pl.BlockSpec((4, 64, 128), lambda _: (0, 0, 0)), pl.BlockSpec((576, 128), lambda _: (0, 0)), sums, sums,
-        ],
-        out_specs=(whole, whole),
+        in_specs=[VMEM] * 6,
+        out_specs=(VMEM, VMEM),
     )
 
 

time: 95.6 us -> 88.7 us (0.928)
  the two profiles are of different devices: /device:TPU:32 before, /device:TPU:71 now
where the time goes in v3:
time: 88.7 us; the launch traced here: 87.9 us
  starting transfers between devices  48.8 us (55%)
  blocking collectives  12.5 us (14%)
  Pallas kernels  12.3 us (14%)
  waiting for transfers between devices  10 us (11%)
  local copies, waits for them, and re-layouts  2.62 us (3%)
    ppermute x1, starting transfers between devices, per_device(): lax.ppermute(jnp.where((section == 1) | (section == 5), edge_rows[1], edg...  13 us
    all_to_all x1, blocking collectives, swap_members(): lax.all_to_all(value, 'inst', 0, 0, tiled=True, axis_index_groups=GROUPS)  12.5 us
    pallas_call x7, Pallas kernels, call(): pl.pallas_call(kernel, name=name, cost_estimate=estimate, **options)  12.3 us
    ppermute x1, starting transfers between devices, per_device(): crossed = lax.ppermute(crossing, 'inst', PARTNER)  10.3 us
    all_to_all x2, starting transfers between devices, swap_members(): lax.all_to_all(value, 'inst', 0, 0, tiled=True, axis_index_groups=GROUPS)  10.2 us
    ppermute x1, waiting for transfers between devices, per_device(): crossed = lax.ppermute(crossing, 'inst', PARTNER)  7.33 us
    ppermute x1, starting transfers between devices, per_device(): arrived_half = lax.ppermute(half, 'inst', PARTNER)  4.56 us
    ppermute x1, starting transfers between devices, per_device(): from_up = lax.ppermute(edge_rows[1], 'row', [(i, i + 1) for i in range(7)])  3.57 us
  transfers between devices with their start and end apart: 9, of which 2 were waited for; matrix products, arithmetic and copies ran while one was open for 2% of the time, Pallas kernels for 9%

profile of v3, /device:TPU:71, one launch (start us, length us, event | category | flops | bytes accessed | tf_op | source)
XLA Modules:
  0.0 87.9 jit_solution(10132747466263324772)
XLA Ops:
  0.6 1.9 %split.1 = (f32[1024,128]{1,0:T(8,128)}, f32[2,4,4,128]{3,2,1,0:T(4,128)}) custom-call(f32[4,4,64,128]{3,2,1,0:T(8,128)} %state.1), custom_call_target="tpu_custom_call" | custom-call | flops 1000 | bytes 1000 | tf_op jit(solution)/shard_map/split/pallas_call | solution.py:267
  2.5 5.3 %all-to-all-start.2 = ((f32[8,128,128]{2,1,0:T(8,128)}), f32[8,128,128]{2,1,0:T(8,128)S(1)}, u32[]{:S(2)}, u32[]{:S(2)}) async-start(f32[8,128,128]{2,1,0:T(8,128)} %bitcast.33), calls=%async_computation.2 | async-start | bytes 1048576 | tf_op jit(solution)/shard_map/all_to_all | solution.py:19
  7.8 1.9 %collective-permute-start.3 = (f32[4,4,128]{2,1,0:T(4,128)S(1)}, f32[4,4,128]{2,1,0:T(4,128)S(1)}, u32[]{:S(2)}, u32[]{:S(2)}) collective-permute-start(f32[4,4,128]{2,1,0:T(4,128)S(1)} %get-tuple-element.109), channel_id=1, source_target_pairs={{64,0},{128,64},{192,128},{256,192},{320,256},{384,320},{448,384},... | collective-permute-start | bytes 24584 | tf_op jit(solution)/shard_map/ppermute | solution.py:287
  9.7 3.6 %collective-permute-start.2 = (f32[4,4,128]{2,1,0:T(4,128)S(1)}, f32[4,4,128]{2,1,0:T(4,128)S(1)}, u32[]{:S(2)}, u32[]{:S(2)}) collective-permute-start(f32[4,4,128]{2,1,0:T(4,128)S(1)} %get-tuple-element.110), channel_id=1, source_target_pairs={{0,64},{64,128},{128,192},{192,256},{256,320},{320,384},{384,448},... | collective-permute-start | bytes 24584 | tf_op jit(solution)/shard_map/ppermute | solution.py:286
  13.3 13.0 %collective-permute-start.4 = (f32[4,4,128]{2,1,0:T(4,128)S(1)}, f32[4,4,128]{2,1,0:T(4,128)S(1)}, u32[]{:S(2)}, u32[]{:S(2)}) collective-permute-start(f32[4,4,128]{2,1,0:T(4,128)S(1)} %broadcast_select_fusion.1), channel_id=1, source_target_pairs={{64,136},{68,140},{72,128},{76,132},{80,152},{84,156},{88,144},{92... | collective-permute-start | bytes 24584 | tf_op jit(solution)/shard_map/ppermute | solution.py:289
  26.3 0.7 half.1
  27.1 4.6 %collective-permute-start.5 = (f32[512,128]{1,0:T(8,128)}, f32[512,128]{1,0:T(8,128)S(1)}, u32[]{:S(2)}, u32[]{:S(2)}) collective-permute-start(f32[512,128]{1,0:T(8,128)} %half.1), channel_id=1, source_target_pairs={{0,8},{4,12},{8,0},{12,4},{16,24},{20,28},{24,16},{28,20},{32,40},... | collective-permute-start | bytes 786440 | tf_op jit(solution)/shard_map/ppermute | solution.py:298
  31.7 14.6 %conditional.2 = (f32[576,128]{1,0:T(8,128)}, f32[512,128]{1,0:T(8,128)S(1)}) conditional(s32[]{:T(128)} %convert_element_type.2, () %tuple.24, (f32[64,64]{1,0:T(8,128)S(1)}, f32[1024,128]{1,0:T(8,128)S(1)}, f32[4,4,128]{2,1,0:T(4,128)S(1)}, f32[4,4,128]{2,1,0:T(4,128)S(1)}, f32[4,4,128]{2,1,0:T(4,128)S(1)}) %tuple.53), branch_computations={%region_0.1_spmd, %region_1.2_spmd} | conditional | flops 2000 | bytes 591840 | solution.py:272
  31.7 1.1 %outgoing.1 = f32[576,128]{1,0:T(8,128)} custom-call(f32[64,64]{1,0:T(8,128)S(1)} %get-tuple-element.22.matrix, f32[1024,128]{1,0:T(8,128)S(1)} %get-tuple-element.23.source, f32[4,4,128]{2,1,0:T(4,128)S(1)} %get-tuple-element.24.up, f32[4,4,128]{2,1,0:T(4,128)S(1)} %get-tuple-element.25.down, f32[4,4,128]{2,1,0:T(4,128)S(1)} %get-tuple-element.26.partner), custom_call_target="tpu_custom_call" | custom-call | flops 1000 | bytes 1000 | tf_op jit(solution)/shard_map/cond/branch_1_fun/outgoing/pallas_call | solution.py:267
  32.8 12.5 %all_to_all.28 = f32[8,72,128]{2,1,0:T(8,128)} all-to-all(f32[8,72,128]{2,1,0:T(8,128)} %bitcast.32), channel_id=1, replica_groups={{0,4,16,20,32,36,48,52},{8,12,24,28,40,44,56,60},{1,5,17,21,33,37,49,53..., dimensions={0} | all-to-all | bytes 589824 | tf_op jit(solution)/shard_map/cond/branch_1_fun/all_to_all | solution.py:19
  45.3 1.0 %pack.1 = f32[512,128]{1,0:T(8,128)S(1)} custom-call(f32[576,128]{1,0:T(8,128)} %bitcast.1.returned), custom_call_target="tpu_custom_call" | custom-call | flops 1000 | bytes 1000 | tf_op jit(solution)/shard_map/cond/branch_1_fun/pack/pallas_call | solution.py:267
  46.3 10.3 %collective-permute-start.6 = (f32[512,128]{1,0:T(8,128)S(1)}, f32[512,128]{1,0:T(8,128)S(1)}, u32[]{:S(2)}, u32[]{:S(2)}) collective-permute-start(f32[512,128]{1,0:T(8,128)S(1)} %get-tuple-element.50), channel_id=1, source_target_pairs={{0,8},{4,12},{8,0},{12,4},{16,24},{20,28},{24,16},{28,20},{32,40},... | collective-permute-start | bytes 786440 | tf_op jit(solution)/shard_map/ppermute | solution.py:314
  56.6 0.6 copy-done.8
  57.3 20.2 %conditional.3 = (f32[1088,128]{1,0:T(8,128)}, f32[4,4,64,128]{3,2,1,0:T(8,128)S(1)}, f32[4,64,128]{2,1,0:T(8,128)S(1)}) conditional(s32[]{:T(128)} %convert_element_type.2, () %tuple.23, (f32[64,64]{1,0:T(8,128)S(1)}, s32[64,64]{1,0:T(8,128)S(1)}, f32[1024,128]{1,0:T(8,128)S(1)}, f32[576,128]{1,0:T(8,128)}, f32[512,128]{1,0:T(8,128)S(1)}, ...), branch_computations={%region_2.3_spmd, %region_3.4_spmd} | conditional | flops 22736 | bytes 2890442 | solution.py:272
  57.3 0.7 select_add_fusion.resample
  58.0 2.6 %arrived.1 = f32[1088,128]{1,0:T(8,128)} custom-call(f32[64,64]{1,0:T(8,128)S(1)} %get-tuple-element.27.matrix, f32[64,64]{1,0:T(8,128)} %select_add_fusion.resample, f32[1024,128]{1,0:T(8,128)S(1)} %get-tuple-element.29.mixed, f32[576,128]{1,0:T(8,128)} %get-tuple-element.30.returned, f32[512,128]{1,0:T(8,128)S(1)} %get-tuple-element.31.source), custom_call_target="tpu_custom_call" | custom-call | flops 1000 | bytes 1000 | tf_op jit(solution)/shard_map/cond/branch_1_fun/arrived/pallas_call | solution.py:267
  60.6 4.9 %all-to-all-start.1 = ((f32[8,136,128]{2,1,0:T(8,128)}), f32[8,136,128]{2,1,0:T(8,128)}, u32[]{:S(2)}, u32[]{:S(2)}) async-start(f32[8,136,128]{2,1,0:T(8,128)} %bitcast.31), calls=%async_computation.1 | async-start | bytes 1114112 | tf_op jit(solution)/shard_map/cond/branch_1_fun/all_to_all | solution.py:19
  66.1 2.1 %collective-permute-start = (f32[4,4,64]{2,1,0:T(4,128)S(1)}, f32[4,4,64]{2,1,0:T(4,128)S(1)}, u32[]{:S(2)}, u32[]{:S(2)}) collective-permute-start(f32[4,4,64]{2,1,0:T(4,128)S(1)} %get-tuple-element.105.last_column), channel_id=1, source_target_pairs={{0,1},{1,2},{2,3},{3,0},{4,5},{5,6},{6,7},{7,4},{8,9},{9,10},{10,1... | collective-permute-start | bytes 12296 | tf_op jit(solution)/shard_map/cond/branch_1_fun/ppermute | solution.py:328
  68.2 3.2 %collective-permute-start.1 = (f32[4,4,64]{2,1,0:T(4,128)S(1)}, f32[4,4,64]{2,1,0:T(4,128)S(1)}, u32[]{:S(2)}, u32[]{:S(2)}) collective-permute-start(f32[4,4,64]{2,1,0:T(4,128)S(1)} %get-tuple-element.106.first_column), channel_id=1, source_target_pairs={{1,0},{2,1},{3,2},{0,3},{5,4},{6,5},{7,6},{4,7},{9,8},{10,9},{11,1... | collective-permute-start | bytes 12296 | tf_op jit(solution)/shard_map/cond/branch_1_fun/ppermute | solution.py:329
  71.5 2.7 %collective-permute-done.1.from_right = f32[4,4,64]{2,1,0:T(4,128)S(1)} collective-permute-done((f32[4,4,64]{2,1,0:T(4,128)S(1)}, f32[4,4,64]{2,1,0:T(4,128)S(1)}, u32[]{:S(2)}, u32[]{:S(2)}) %collective-permute-start.1) | collective-permute-done | bytes 4128 | tf_op jit(solution)/shard_map/cond/branch_1_fun/ppermute | solution.py:329
  74.8 2.7 %spatial.1 = (f32[4,4,64,128]{3,2,1,0:T(8,128)S(1)}, f32[4,64,128]{2,1,0:T(8,128)S(1)}) custom-call(f32[4,4,64,128]{3,2,1,0:T(8,128)S(1)} %get-tuple-element.79.state, f32[4,4,64]{2,1,0:T(4,128)} %copy-done.5, f32[4,4,64]{2,1,0:T(4,128)} %copy-done.4, f32[4,4,64]{2,1,0:T(4,128)} %copy-done.6, f32[4,4,64]{2,1,0:T(4,128)} %copy-done.7), custom_call_target="tpu_custom_call" | custom-call | flops 1000 | bytes 1000 | tf_op jit(solution)/shard_map/cond/branch_1_fun/spatial/pallas_call | solution.py:267
  77.5 7.3 %collective-permute-done.6.crossed = f32[512,128]{1,0:T(8,128)S(1)} collective-permute-done((f32[512,128]{1,0:T(8,128)S(1)}, f32[512,128]{1,0:T(8,128)S(1)}, u32[]{:S(2)}, u32[]{:S(2)}) %collective-permute-start.6) | collective-permute-done | bytes 262176 | tf_op jit(solution)/shard_map/ppermute | solution.py:314
  84.8 0.7 copy-done.1
  85.5 2.4 %final.1 = (f32[4,4,64,128]{3,2,1,0:T(8,128)}, f32[4,4,64,128]{3,2,1,0:T(8,128)}) custom-call(f32[4,4,64,128]{3,2,1,0:T(8,128)} %base.1, f32[2,4,4,128]{3,2,1,0:T(4,128)} %get-tuple-element.44.edges, f32[4,4,64,128]{3,2,1,0:T(8,128)S(1)} %get-tuple-element.47.spatial, f32[4,64,128]{2,1,0:T(8,128)S(1)} %get-tuple-element.48.step, ...), custom_call_target="tpu_custom_call" | custom-call | flops 1000 | bytes 1000 | tf_op jit(solution)/shard_map/final/pallas_call | solution.py:267
  (33 shorter events, 1.3 us)
Async XLA Ops:
  2.5 5.3 %copy-start.2 = (f32[2,4,4,128]{3,2,1,0:T(4,128)S(1)}, f32[2,4,4,128]{3,2,1,0:T(4,128)}, u32[]{:S(2)}) copy-start(f32[2,4,4,128]{3,2,1,0:T(4,128)} %get-tuple-element.44.edges) | copy-start | bytes 49156
  2.5 23.8 %all-to-all-start.2 = ((f32[8,128,128]{2,1,0:T(8,128)}), f32[8,128,128]{2,1,0:T(8,128)S(1)}, u32[]{:S(2)}, u32[]{:S(2)}) async-start(f32[8,128,128]{2,1,0:T(8,128)} %bitcast.33), calls=%async_computation.2 | async-start | bytes 1048576 | tf_op jit(solution)/shard_map/all_to_all | solution.py:19
  7.8 23.8 %collective-permute-start.3 = (f32[4,4,128]{2,1,0:T(4,128)S(1)}, f32[4,4,128]{2,1,0:T(4,128)S(1)}, u32[]{:S(2)}, u32[]{:S(2)}) collective-permute-start(f32[4,4,128]{2,1,0:T(4,128)S(1)} %get-tuple-element.109), channel_id=1, source_target_pairs={{64,0},{128,64},{192,128},{256,192},{320,256},{384,320},{448,384},... | collective-permute-start | bytes 24584 | tf_op jit(solution)/shard_map/ppermute | solution.py:287
  9.7 21.9 %collective-permute-start.2 = (f32[4,4,128]{2,1,0:T(4,128)S(1)}, f32[4,4,128]{2,1,0:T(4,128)S(1)}, u32[]{:S(2)}, u32[]{:S(2)}) collective-permute-start(f32[4,4,128]{2,1,0:T(4,128)S(1)} %get-tuple-element.110), channel_id=1, source_target_pairs={{0,64},{64,128},{128,192},{192,256},{256,320},{320,384},{384,448},... | collective-permute-start | bytes 24584 | tf_op jit(solution)/shard_map/ppermute | solution.py:286
  13.3 18.3 %collective-permute-start.4 = (f32[4,4,128]{2,1,0:T(4,128)S(1)}, f32[4,4,128]{2,1,0:T(4,128)S(1)}, u32[]{:S(2)}, u32[]{:S(2)}) collective-permute-start(f32[4,4,128]{2,1,0:T(4,128)S(1)} %broadcast_select_fusion.1), channel_id=1, source_target_pairs={{64,136},{68,140},{72,128},{76,132},{80,152},{84,156},{88,144},{92... | collective-permute-start | bytes 24584 | tf_op jit(solution)/shard_map/ppermute | solution.py:289
  26.3 5.3 %copy-start.3 = (f32[1,64,64]{2,1,0:T(8,128)S(1)}, f32[1,64,64]{2,1,0:T(8,128)}, u32[]{:S(2)}) copy-start(f32[1,64,64]{2,1,0:T(8,128)} %param.11) | copy-start | bytes 49156
  27.1 29.5 %collective-permute-start.5 = (f32[512,128]{1,0:T(8,128)}, f32[512,128]{1,0:T(8,128)S(1)}, u32[]{:S(2)}, u32[]{:S(2)}) collective-permute-start(f32[512,128]{1,0:T(8,128)} %half.1), channel_id=1, source_target_pairs={{0,8},{4,12},{8,0},{12,4},{16,24},{20,28},{24,16},{28,20},{32,40},... | collective-permute-start | bytes 786440 | tf_op jit(solution)/shard_map/ppermute | solution.py:298
  31.7 25.0 %copy-start = (f32[4,4,64,128]{3,2,1,0:T(8,128)S(1)}, f32[4,4,64,128]{3,2,1,0:T(8,128)}, u32[]{:S(2)}) copy-start(f32[4,4,64,128]{3,2,1,0:T(8,128)} %state.1) | copy-start | bytes 1572868
  46.3 38.6 %collective-permute-start.6 = (f32[512,128]{1,0:T(8,128)S(1)}, f32[512,128]{1,0:T(8,128)S(1)}, u32[]{:S(2)}, u32[]{:S(2)}) collective-permute-start(f32[512,128]{1,0:T(8,128)S(1)} %get-tuple-element.50), channel_id=1, source_target_pairs={{0,8},{4,12},{8,0},{12,4},{16,24},{20,28},{24,16},{28,20},{32,40},... | collective-permute-start | bytes 786440 | tf_op jit(solution)/shard_map/ppermute | solution.py:314
  56.6 0.7 copy-start.8
  56.6 0.7 copy-start.9
  60.6 16.9 %all-to-all-start.1 = ((f32[8,136,128]{2,1,0:T(8,128)}), f32[8,136,128]{2,1,0:T(8,128)}, u32[]{:S(2)}, u32[]{:S(2)}) async-start(f32[8,136,128]{2,1,0:T(8,128)} %bitcast.31), calls=%async_computation.1 | async-start | bytes 1114112 | tf_op jit(solution)/shard_map/cond/branch_1_fun/all_to_all | solution.py:19
  66.1 8.0 %copy-start.4 = (f32[4,4,64]{2,1,0:T(4,128)}, f32[4,4,64]{2,1,0:T(4,128)S(1)}, u32[]{:S(2)}) copy-start(f32[4,4,64]{2,1,0:T(4,128)S(1)} %get-tuple-element.105.last_column) | copy-start | bytes 12292 | tf_op jit(solution)/shard_map/cond
  66.1 8.0 %copy-start.5 = (f32[4,4,64]{2,1,0:T(4,128)}, f32[4,4,64]{2,1,0:T(4,128)S(1)}, u32[]{:S(2)}) copy-start(f32[4,4,64]{2,1,0:T(4,128)S(1)} %get-tuple-element.106.first_column) | copy-start | bytes 12292 | tf_op jit(solution)/shard_map/cond
  66.1 5.3 %collective-permute-start = (f32[4,4,64]{2,1,0:T(4,128)S(1)}, f32[4,4,64]{2,1,0:T(4,128)S(1)}, u32[]{:S(2)}, u32[]{:S(2)}) collective-permute-start(f32[4,4,64]{2,1,0:T(4,128)S(1)} %get-tuple-element.105.last_column), channel_id=1, source_target_pairs={{0,1},{1,2},{2,3},{3,0},{4,5},{5,6},{6,7},{7,4},{8,9},{9,10},{10,1... | collective-permute-start | bytes 12296 | tf_op jit(solution)/shard_map/cond/branch_1_fun/ppermute | solution.py:328
  68.2 5.9 %collective-permute-start.1 = (f32[4,4,64]{2,1,0:T(4,128)S(1)}, f32[4,4,64]{2,1,0:T(4,128)S(1)}, u32[]{:S(2)}, u32[]{:S(2)}) collective-permute-start(f32[4,4,64]{2,1,0:T(4,128)S(1)} %get-tuple-element.106.first_column), channel_id=1, source_target_pairs={{1,0},{2,1},{3,2},{0,3},{5,4},{6,5},{7,6},{4,7},{9,8},{10,9},{11,1... | collective-permute-start | bytes 12296 | tf_op jit(solution)/shard_map/cond/branch_1_fun/ppermute | solution.py:329
  71.4 2.7 %copy-start.6 = (f32[4,4,64]{2,1,0:T(4,128)}, f32[4,4,64]{2,1,0:T(4,128)S(1)}, u32[]{:S(2)}) copy-start(f32[4,4,64]{2,1,0:T(4,128)S(1)} %collective-permute-done.from_left) | copy-start | bytes 12292 | tf_op jit(solution)/shard_map/cond
  74.2 0.6 copy-start.7
  84.8 0.7 copy-start.1
